TPU v7x, 512 devices: a whole 4x8x8 slice. The times are simulated.
512 devices in a mesh: tile: 64 (over y_lo, z, core), kern: 8 (over x, y_hi).
Axes of the slice: x: 4, y: 8 (y_hi: 2, y_lo: 4; y = y_hi * 4 + y_lo), z: 8, core: 2. Of those that a mesh axis runs over, the one named last changes fastest.
Arguments:
- mask_tile: float32 [64, 256, 256], P('tile'), may hold values from 0 to 1
- kernels: float32 [2, 24, 128, 128], P(None, 'kern'), may hold values from -0.03125 to 0.03125
- socs_weight: float32 [24], P('kern'), may hold values from 0.1 to 1
- adjacency: int32 [64, 2], P('tile'), may hold values from 0 to 1, as said below
- target: int32 [64, 256, 256], P('tile'), may hold values 0 or 1
Outputs:
- resist: float32 [64, 256, 256], P('tile')
- mask_grad: float32 [64, 256, 256], P('tile')
Inputs may be any that keep to these rules, and one draw needn't show every extreme that they name: `adjacency`: every tile in an even column of the grid, or in column 3, is joined to its right neighbour, and every tile in an even row to its lower neighbour; other links are drawn.
All inputs are finite; a program needn't handle non-finite values. No bound on the sum of `target` on one device may be relied on, other than what follows from the above.
Results may differ from a plain program's by a relative error of at most 0.00027.
Values sent between devices are 32-bit elements; how exact they have to be, the bound alone decides.
A program may use at most 64 MiB of HBM per device.

v0:
```python
import functools
import math

import jax
import jax.numpy as jnp
import ml_dtypes
import numpy as np
from jax import lax
from jax.experimental import pallas as pl
from jax.experimental.pallas import tpu as pltpu
from jax.sharding import PartitionSpec as P

GRID_W = 8
STEEP = 20.0
THRESH = 0.33
BLK = 128
EXTENT = 3 * BLK
CORE = 2 * BLK
HALO = BLK // 2
HALF_SQRT3 = math.sqrt(3.0) / 2.0
MESH = pl.DeviceIdType.MESH
F32 = jnp.float32
BF16 = jnp.bfloat16


def dft_tables():
    place = np.arange(BLK)
    groups = (3 * place, 3 * place + 1, -(3 * place + 1))
    mats = []
    for freq in groups:
        angle = 2.0 * np.pi * (np.outer(place, freq) % EXTENT) / EXTENT
        c, s = np.cos(angle), -np.sin(angle)
        mats.append(np.block([[c, s], [-s, c]]))
    fwd = np.stack(mats).astype(np.float32)
    both = np.stack([fwd, fwd.transpose(0, 2, 1)])
    high = both.astype(ml_dtypes.bfloat16)
    low = (both - high.astype(np.float32)).astype(ml_dtypes.bfloat16)
    return np.stack([high, low])


def split(x):
    high = x.astype(BF16)
    return high, (x - high.astype(F32)).astype(BF16)


def dot(a, b):
    return jnp.dot(a, b, preferred_element_type=F32)


def mul_right(x, high, low):
    xh, xl = split(x)
    return dot(xh, high) + (dot(xh, low) + dot(xl, high))


def mul_left(high, low, x):
    xh, xl = split(x)
    return dot(high, xh) + (dot(low, xh) + dot(high, xl))


def fwd_mat(tab, g):
    return tab[0, 0, g], tab[1, 0, g]


def t_mat(tab, g):
    return tab[0, 1, g], tab[1, 1, g]


def lanes(re, im):
    return jnp.concatenate([re, im], axis=1)


def rows(re, im):
    return jnp.concatenate([re, im], axis=0)


def responses(kernels, tab, mid, resp):
    scale = 1.0 / (EXTENT * EXTENT)
    re = jnp.concatenate([kernels[0, k] for k in range(3)], axis=1) * scale
    im = jnp.concatenate([kernels[1, k] for k in range(3)], axis=1) * -scale
    taps = rows(re, im)
    for g in range(3):
        out = mul_left(*t_mat(tab, g), taps)
        mid[0, pl.ds(g * BLK, BLK), :] = out[:BLK]
        mid[1, pl.ds(g * BLK, BLK), :] = out[BLK:]
    for k in range(3):
        cols = pl.ds(k * BLK, BLK)
        x = lanes(mid[0, :, cols], mid[1, :, cols])
        for g in range(3):
            out = mul_right(x, *fwd_mat(tab, g))
            resp[k, 0, :, pl.ds(g * BLK, BLK)] = out[:, :BLK]
            resp[k, 1, :, pl.ds(g * BLK, BLK)] = out[:, BLK:]


def spectrum(ext, tab, mid, spec):
    x0, x1, x2 = (ext[:, pl.ds(j * BLK, BLK)] for j in range(3))
    z0 = x0 + x1 + x2
    z1 = lanes(x0 - 0.5 * (x1 + x2), HALF_SQRT3 * (x2 - x1))
    h0, l0 = fwd_mat(tab, 0)
    out0 = mul_right(z0, h0[:BLK], l0[:BLK])
    out1 = mul_right(z1, *fwd_mat(tab, 1))
    mid[0, :, pl.ds(0, BLK)] = out0[:, :BLK]
    mid[1, :, pl.ds(0, BLK)] = out0[:, BLK:]
    mid[0, :, pl.ds(BLK, BLK)] = out1[:, :BLK]
    mid[1, :, pl.ds(BLK, BLK)] = out1[:, BLK:]
    two = pl.ds(0, CORE)
    a_re, b_re, c_re = (mid[0, pl.ds(j * BLK, BLK), two] for j in range(3))
    a_im, b_im, c_im = (mid[1, pl.ds(j * BLK, BLK), two] for j in range(3))
    s_re, s_im = b_re + c_re, b_im + c_im
    e_re, e_im = a_re - 0.5 * s_re, a_im - 0.5 * s_im
    f_re, f_im = HALF_SQRT3 * (b_re - c_re), HALF_SQRT3 * (b_im - c_im)
    z_re, z_im = a_re + s_re, a_im + s_im
    z_re = lanes(z_re, z_re[:, BLK:])
    z_im = lanes(z_im, -z_im[:, BLK:])
    out = mul_left(*t_mat(tab, 0), rows(z_re, z_im))
    spec[0, pl.ds(0, BLK), :] = out[:BLK]
    spec[1, pl.ds(0, BLK), :] = out[BLK:]
    out1 = mul_left(*t_mat(tab, 1), rows(e_re + f_im, e_im - f_re))
    out2 = mul_left(*t_mat(tab, 2), rows(e_re - f_im, e_im + f_re))
    spec[0, pl.ds(BLK, BLK), :] = lanes(out1[:BLK], out2[:BLK, BLK:])
    spec[1, pl.ds(BLK, BLK), :] = lanes(out1[BLK:], -out2[BLK:, BLK:])
    spec[0, pl.ds(2 * BLK, BLK), :] = lanes(out2[:BLK], out1[:BLK, BLK:])
    spec[1, pl.ds(2 * BLK, BLK), :] = lanes(out2[BLK:], -out1[BLK:, BLK:])


def field_of(k, resp, spec, tab, mid, field):
    t = []
    for g in range(3):
        cols = pl.ds(g * BLK, BLK)
        q_re, q_im = resp[k, 0, :, cols], resp[k, 1, :, cols]
        e_re, e_im = spec[0, :, cols], spec[1, :, cols]
        x = lanes(e_re * q_re + e_im * q_im, e_im * q_re - e_re * q_im)
        t.append(mul_right(x, *t_mat(tab, g)))
    s, d = t[1] + t[2], HALF_SQRT3 * (t[1] - t[2])
    first, e = t[0] + s, t[0] - 0.5 * s
    mid[0, :, pl.ds(0, BLK)] = first[:, :BLK]
    mid[1, :, pl.ds(0, BLK)] = first[:, BLK:]
    mid[0, :, pl.ds(BLK, BLK)] = e[:, :BLK] - d[:, BLK:]
    mid[1, :, pl.ds(BLK, BLK)] = e[:, BLK:] + d[:, :BLK]
    t = []
    for g in range(3):
        block = pl.ds(g * BLK, BLK)
        x = rows(mid[0, block, pl.ds(0, CORE)], mid[1, block, pl.ds(0, CORE)])
        t.append(mul_left(*fwd_mat(tab, g), x))
    s, d = t[1] + t[2], HALF_SQRT3 * (t[1] - t[2])
    first, e = t[0] + s, t[0] - 0.5 * s
    field[k, 0, pl.ds(0, BLK), :] = first[:BLK]
    field[k, 1, pl.ds(0, BLK), :] = first[BLK:]
    field[k, 0, pl.ds(BLK, BLK), :] = e[:BLK] - d[BLK:]
    field[k, 1, pl.ds(BLK, BLK), :] = e[BLK:] + d[:BLK]


def grad_of(k, factor, slope, field, resp, tab, mid, acc):
    scaled = factor * slope[...]
    s_re, s_im = scaled * field[k, 0], scaled * field[k, 1]
    a_re, a_im, b_re, b_im = s_re[:BLK], s_im[:BLK], s_re[BLK:], s_im[BLK:]
    e_re, e_im = a_re - 0.5 * b_re, a_im - 0.5 * b_im
    f_re, f_im = HALF_SQRT3 * b_re, HALF_SQRT3 * b_im
    z = (
        rows(a_re + b_re, a_im + b_im),
        rows(e_re + f_im, e_im - f_re),
        rows(e_re - f_im, e_im + f_re),
    )
    for g in range(3):
        out = mul_left(*t_mat(tab, g), z[g])
        mid[0, pl.ds(g * BLK, BLK), pl.ds(0, CORE)] = out[:BLK]
        mid[1, pl.ds(g * BLK, BLK), pl.ds(0, CORE)] = out[BLK:]
    first, second = pl.ds(0, BLK), pl.ds(BLK, BLK)
    a_re, a_im, b_re, b_im = mid[0, :, first], mid[1, :, first], mid[0, :, second], mid[1, :, second]
    e_re, e_im = a_re - 0.5 * b_re, a_im - 0.5 * b_im
    f_re, f_im = HALF_SQRT3 * b_re, HALF_SQRT3 * b_im
    z = (
        lanes(a_re + b_re, a_im + b_im),
        lanes(e_re + f_im, e_im - f_re),
        lanes(e_re - f_im, e_im + f_re),
    )
    for g in range(3):
        cols = pl.ds(g * BLK, BLK)
        out = mul_right(z[g], *fwd_mat(tab, g))
        o_re, o_im = out[:, :BLK], out[:, BLK:]
        q_re, q_im = resp[k, 0, :, cols], resp[k, 1, :, cols]
        acc[0, :, cols] += o_re * q_re - o_im * q_im
        acc[1, :, cols] += o_re * q_im + o_im * q_re


def ext_gradient(acc, tab, mid):
    p0, p1, p2 = (pl.ds(g * BLK, BLK) for g in range(3))
    t0 = mul_left(*fwd_mat(tab, 0), rows(acc[0, p0, :], acc[1, p0, :]))
    t0_re, t0_im = t0[:BLK], t0[BLK:]
    t0_re = lanes(t0_re[:, :BLK], t0_re[:, BLK:CORE] + t0_re[:, CORE:])
    t0_im = lanes(t0_im[:, :BLK], t0_im[:, BLK:CORE] - t0_im[:, CORE:])
    x_re = lanes(acc[0, p1, p0], acc[0, p1, p1] + acc[0, p2, p2])
    x_im = lanes(acc[1, p1, p0], acc[1, p1, p1] - acc[1, p2, p2])
    t1 = mul_left(*fwd_mat(tab, 1), rows(x_re, x_im))
    x_re = lanes(acc[0, p2, p0], acc[0, p2, p1] + acc[0, p1, p2])
    x_im = lanes(acc[1, p2, p0], acc[1, p2, p1] - acc[1, p1, p2])
    t2 = mul_left(*fwd_mat(tab, 2), rows(x_re, x_im))
    s, d = t1 + t2, HALF_SQRT3 * (t1 - t2)
    e_re, e_im = t0_re - 0.5 * s[:BLK], t0_im - 0.5 * s[BLK:]
    two = pl.ds(0, CORE)
    mid[0, p0, two], mid[1, p0, two] = t0_re + s[:BLK], t0_im + s[BLK:]
    mid[0, p1, two], mid[1, p1, two] = e_re - d[BLK:], e_im + d[:BLK]
    mid[0, p2, two], mid[1, p2, two] = e_re + d[BLK:], e_im - d[:BLK]
    h0, l0 = t_mat(tab, 0)
    r0 = mul_right(lanes(mid[0, :, p0], mid[1, :, p0]), h0[:, :BLK], l0[:, :BLK])
    r1 = mul_right(lanes(mid[0, :, p1], mid[1, :, p1]), *t_mat(tab, 1))
    e, d = r0 - 0.5 * r1[:, :BLK], HALF_SQRT3 * r1[:, BLK:]
    return r0 + r1[:, :BLK], e - d, e + d


def body_kernel(
    mask, kernels, target, tab, weight, link, resist_out, grad_out,
    mid, resp, spec, field, acc, ext, side_out, side_in, vert_out, vert_in,
    clear_in, clear_sum, clear_far, power, power_in, power_mine, power_far, power_all, slope,
    grad_parts, grad_in, grad_sum, grad_far, owned, fold_out, fold_in, edge_out, edge_in, gathered,
    side_send, side_recv, vert_send, vert_recv, share_send, share_recv,
    clear_send, clear_recv, cfar_send, cfar_recv,
    psc_send, psc_recv, pfar_send, pfar_recv, pall_send, pall_recv,
    gsc_send, gsc_recv, gfar_send, gfar_recv, fold_send, fold_recv,
    edge_send, edge_recv, near_send, near_recv, all_send, all_recv,
):
    tile = lax.axis_index("tile")
    kern = lax.axis_index("kern")
    tiles = lax.axis_size("tile")
    x = kern // 2
    half = kern % 2
    column = (tile + GRID_W // 2) % GRID_W
    right_ok = jnp.where((column < GRID_W - 1) & (tile + 1 < tiles), 1.0, 0.0)
    down_ok = jnp.where(tile + GRID_W < tiles, 1.0, 0.0)
    right_link = link[0, 0].astype(F32) * right_ok
    down_link = link[0, 1].astype(F32) * down_ok

    def at(tile_by, kern_index):
        return {"tile": (tile + tile_by + tiles) % tiles, "kern": kern_index}

    right, left, below, above = at(1, kern), at(-1, kern), at(GRID_W, kern), at(-GRID_W, kern)
    far = at(0, 2 * x + 1 - half)
    x_at = [(x + d) % 4 for d in range(4)]
    peers = [at(0, 2 * x_at[d] + half) for d in range(4)]
    corner_tile = jnp.where((x == 0) | (x == 2), -GRID_W, GRID_W)
    cross = at(corner_tile, 2 * (x + 1 - 2 * (x % 2)) + half)

    barrier = pltpu.get_barrier_semaphore()
    partners = [right, left, below, above, far, cross] + peers[1:]
    for one in partners:
        pl.semaphore_signal(barrier, inc=1, device_id=one, device_id_type=MESH)

    def remote(src, dst, send, recv, device):
        return pltpu.make_async_remote_copy(
            src_ref=src, dst_ref=dst, send_sem=send, recv_sem=recv, device_id=device, device_id_type=MESH
        )

    lane = lax.broadcasted_iota(jnp.int32, (BLK, BLK), 1) < HALO
    lane_all = lax.broadcasted_iota(jnp.int32, (CORE, BLK), 1) < HALO

    a0, a1 = mask[0, :, pl.ds(0, BLK)], mask[0, :, pl.ds(BLK, BLK)]
    r0, r1 = pltpu.roll(a0, HALO, 1), pltpu.roll(a1, HALO, 1)
    outer = jnp.where(lane_all, r1, r0)
    inner = jnp.where(lane_all, r0, r1)
    flipped = pltpu.roll(outer, HALO, 1)
    side_out[0] = jnp.where(lane, outer[:BLK], flipped[BLK:]) * right_link
    side_out[1] = jnp.where(lane, flipped[:BLK], outer[BLK:])
    taps = [[jnp.sum(kernels[c, k], keepdims=True) for k in range(3)] for c in range(2)]
    clear_part = sum(weight[k] * (taps[0][k] * taps[0][k] + taps[1][k] * taps[1][k]) for k in range(3))
    clear_in[x] = jnp.broadcast_to(clear_part, (8, BLK))

    pl.semaphore_wait(barrier, len(partners))
    to_right = remote(side_out.at[0], side_in.at[0], side_send.at[0], side_recv.at[0], right)
    to_left = remote(side_out.at[1], side_in.at[1], side_send.at[1], side_recv.at[1], left)
    to_right.start()
    to_left.start()
    clear_copies = [
        remote(clear_in.at[x], clear_in.at[x], clear_send.at[d - 1], clear_recv.at[d - 1], peers[d])
        for d in range(1, 4)
    ]
    for copy in clear_copies:
        copy.start()

    middle = pl.ds(HALO, CORE)
    ext[middle, pl.ds(BLK, BLK)] = inner
    to_right.wait_recv()
    to_left.wait_recv()
    from_left, from_right = side_in[0], side_in[1] * right_link
    upper, lower = pl.ds(HALO, BLK), pl.ds(HALO + BLK, BLK)
    ext[upper, pl.ds(0, BLK)] = jnp.where(lane, from_left, outer[:BLK])
    ext[lower, pl.ds(0, BLK)] = jnp.where(lane, pltpu.roll(from_left, HALO, 1), outer[BLK:])
    ext[upper, pl.ds(CORE, BLK)] = jnp.where(lane, outer[:BLK], pltpu.roll(from_right, HALO, 1))
    ext[lower, pl.ds(CORE, BLK)] = jnp.where(lane, outer[BLK:], from_right)

    part = HALO // 4
    vert_out[0] = ext[pl.ds(pl.multiple_of(CORE + part * x, part), part), :] * down_link
    vert_out[1] = ext[pl.ds(pl.multiple_of(HALO + part * x, part), part), :]
    to_below = remote(vert_out.at[0], vert_in.at[x, 0], vert_send.at[0], vert_recv.at[0], below)
    to_above = remote(vert_out.at[1], vert_in.at[x, 1], vert_send.at[1], vert_recv.at[1], above)
    to_below.start()
    to_above.start()

    responses(kernels, tab, mid, resp)

    to_below.wait_recv()
    to_above.wait_recv()
    shares = [
        remote(vert_in.at[x], vert_in.at[x], share_send.at[d - 1], share_recv.at[d - 1], peers[d])
        for d in range(1, 4)
    ]
    for copy in shares:
        copy.start()
    for copy in clear_copies:
        copy.wait_recv()
    clear_sum[...] = clear_in[0] + clear_in[1] + clear_in[2] + clear_in[3]
    clear_copy = remote(clear_sum, clear_far, cfar_send, cfar_recv, far)
    clear_copy.start()
    for copy in shares:
        copy.wait_recv()
    for q in range(4):
        ext[pl.ds(part * q, part), :] = vert_in[q, 0]
        ext[pl.ds(HALO + CORE + part * q, part), :] = vert_in[q, 1] * down_link

    spectrum(ext, tab, mid, spec)

    def field_step(k, carry):
        field_of(k, resp, spec, tab, mid, field)
        return carry

    lax.fori_loop(0, 3, field_step, 0)
    for q in range(4):
        block = pl.ds(q * HALO, HALO)
        power[q] = sum(
            weight[k] * (field[k, 0, block, :] * field[k, 0, block, :] + field[k, 1, block, :] * field[k, 1, block, :])
            for k in range(3)
        )

    scatter = [
        remote(power.at[x_at[d]], power_in.at[d - 1], psc_send.at[d - 1], psc_recv.at[d - 1], peers[d])
        for d in range(1, 4)
    ]
    for copy in scatter:
        copy.start()
    acc[...] = jnp.zeros_like(acc)
    clear_copy.wait_recv()
    for copy in scatter:
        copy.wait_recv()
    power_mine[...] = power[x] + power_in[0] + power_in[1] + power_in[2]
    swap = remote(power_mine, power_far, pfar_send, pfar_recv, far)
    swap.start()
    swap.wait_recv()
    power_all[x] = power_mine[...] + power_far[...]
    gather = [
        remote(power_all.at[x], power_all.at[x], pall_send.at[d - 1], pall_recv.at[d - 1], peers[d])
        for d in range(1, 4)
    ]
    for copy in gather:
        copy.start()
    for copy in gather:
        copy.wait_recv()
    clear = (clear_sum[...] + clear_far[...])[0:1, 0:1]
    for q in range(4):
        block = pl.ds(q * HALO, HALO)
        intensity = power_all[q] / clear
        resist = 1.0 / (1.0 + jnp.exp(-STEEP * (intensity - THRESH)))
        resist_out[0, block, :] = resist
        wanted = target[0, block, :].astype(F32)
        slope[block, :] = (4.0 * STEEP) * (resist - wanted) * resist * (1.0 - resist) / clear

    def grad_step(k, carry):
        grad_of(k, weight[k], slope, field, resp, tab, mid, acc)
        return carry

    lax.fori_loop(0, 3, grad_step, 0)
    blocks = ext_gradient(acc, tab, mid)
    bits = [(HALO + 64 * q + 32 * h, q, h, 0, 32) for q in range(4) for h in range(2)]
    bits += [(EXTENT - HALO + 32 * h + 16 * q, q, h, 32, 16) for q in range(2) for h in range(2)]
    bits += [(32 * h + 16 * (3 - q), q, h, 32, 16) for q in (2, 3) for h in range(2)]
    for c in range(3):
        for start, q, h, to, count in bits:
            grad_parts[q, h, pl.ds(to, count), pl.ds(c * BLK, BLK)] = blocks[c][start : start + count]

    scatter = [
        remote(grad_parts.at[x_at[d]], grad_in.at[d - 1], gsc_send.at[d - 1], gsc_recv.at[d - 1], peers[d])
        for d in range(1, 4)
    ]
    for copy in scatter:
        copy.start()
    for copy in scatter:
        copy.wait_recv()
    grad_sum[...] = grad_parts[x] + grad_in[0] + grad_in[1] + grad_in[2]
    swap2 = remote(grad_sum.at[1 - half], grad_far, gfar_send, gfar_recv, far)
    swap2.start()
    swap2.wait_recv()
    total = grad_sum[half] + grad_far[...]

    low_x = x < 2
    fold_out[...] = total[32:] * jnp.where(low_x, down_link, 1.0)
    owned[...] = total[:32]
    slot = jnp.where((x == 1) | (x == 2), 1, 0)
    fold_copy = remote(
        fold_out, fold_in.at[slot], fold_send, fold_recv.at[slot],
        at(jnp.where(low_x, GRID_W, -GRID_W), jnp.where(low_x, 0, 6) + half),
    )
    fold_copy.start()

    @pl.when((x == 0) | (x == 3))
    def _():
        factor = jnp.where(x == 0, 1.0, down_link)
        for s in range(2):
            remote(fold_out, fold_in.at[s], fold_send, fold_recv.at[s], far).wait_recv()
        for s in range(2):
            owned[pl.ds(16 * s, 16), :] += fold_in[s] * factor

    edge_out[0] = owned[:, pl.ds(CORE, BLK)] * right_link
    edge_out[1] = owned[:, pl.ds(0, BLK)]
    edges = [
        remote(edge_out.at[0], edge_in.at[0], edge_send.at[0], edge_recv.at[0], right),
        remote(edge_out.at[1], edge_in.at[1], edge_send.at[1], edge_recv.at[1], left),
    ]
    for copy in edges:
        copy.start()
    for copy in edges:
        copy.wait_recv()
    near_lane = lax.broadcasted_iota(jnp.int32, (32, BLK), 1) < HALO
    b0 = owned[:, pl.ds(0, BLK)] + edge_in[0]
    b1 = owned[:, pl.ds(BLK, BLK)]
    b2 = owned[:, pl.ds(CORE, BLK)] + edge_in[1] * right_link
    c0, c1, c2 = (pltpu.roll(b, HALO, 1) for b in (b0, b1, b2))
    gathered[x, half] = lanes(jnp.where(near_lane, c0, c1), jnp.where(near_lane, c1, c2))

    mine = gathered.at[x, half]
    near = remote(mine, mine, near_send, near_recv, far)
    near.start()
    near.wait_recv()
    finals = [
        remote(gathered.at[x], gathered.at[x], all_send.at[d - 1], all_recv.at[d - 1], peers[d])
        for d in range(1, 4)
    ]
    for copy in finals:
        copy.start()
    for copy in finals:
        copy.wait_recv()
    for q in range(4):
        for h in range(2):
            grad_out[0, pl.ds(64 * q + 32 * h, 32), :] = gathered[q, h]

    sent = [to_right, to_left, to_below, to_above, clear_copy, swap, swap2, fold_copy, near]
    for copy in sent + clear_copies + shares + gather + edges + finals:
        copy.wait_send()
    for d in range(1, 4):
        remote(power.at[x], power_in.at[d - 1], psc_send.at[d - 1], psc_recv.at[d - 1], peers[d]).wait_send()
    for copy in scatter:
        copy.wait_send()


def body(mask, kernels, weight, link, target):
    vmem = pl.BlockSpec(memory_space=pltpu.VMEM)
    smem = pl.BlockSpec(memory_space=pltpu.SMEM)
    dma = pltpu.SemaphoreType.DMA
    f32 = lambda *shape: pltpu.VMEM(shape, F32)
    scratch = [
        f32(2, EXTENT, EXTENT), f32(3, 2, EXTENT, EXTENT), f32(2, EXTENT, EXTENT), f32(3, 2, CORE, CORE),
        f32(2, EXTENT, EXTENT), f32(EXTENT, EXTENT),
        f32(2, BLK, BLK), f32(2, BLK, BLK), f32(2, 16, EXTENT), f32(4, 2, 16, EXTENT),
        f32(4, 8, BLK), f32(8, BLK), f32(8, BLK),
        f32(4, HALO, CORE), f32(3, HALO, CORE), f32(HALO, CORE), f32(HALO, CORE), f32(4, HALO, CORE), f32(CORE, CORE),
        f32(4, 2, 48, EXTENT), f32(3, 2, 48, EXTENT), f32(2, 48, EXTENT), f32(48, EXTENT),
        f32(32, EXTENT), f32(16, EXTENT), f32(2, 16, EXTENT), f32(2, 32, BLK), f32(2, 32, BLK), f32(4, 2, 32, CORE),
    ]
    scratch += [dma((2,))] * 4 + [dma((3,))] * 4 + [dma] * 2 + [dma((3,))] * 2 + [dma] * 2 + [dma((3,))] * 2
    scratch += [dma((3,))] * 2 + [dma] * 2 + [dma, dma((2,))] + [dma((2,))] * 2 + [dma] * 2 + [dma((3,))] * 2
    out = jax.ShapeDtypeStruct((1, CORE, CORE), F32)
    return pl.pallas_call(
        body_kernel,
        out_shape=(out, out),
        in_specs=[vmem, vmem, vmem, vmem, smem, smem],
        out_specs=(vmem, vmem),
        scratch_shapes=scratch,
        compiler_params=pltpu.CompilerParams(
            collective_id=0, has_side_effects=True, vmem_limit_bytes=48 * 2**20
        ),
    )(mask, kernels, target, jnp.asarray(dft_tables()), weight, link)


def solution(mesh):
    in_specs = (
        P("tile", None, None),
        P(None, "kern", None, None),
        P("kern"),
        P("tile", None),
        P("tile", None, None),
    )
    out_specs = (P("tile", None, None), P("tile", None, None))
    return jax.shard_map(body, mesh=mesh, in_specs=in_specs, out_specs=out_specs, check_vma=False)
```

profile of v0, /device:TPU:1, one launch (start us, length us, event | category | flops | bytes accessed | tf_op | source)
XLA Modules:
  0.0 92.8 jit_solution(11194050290833561281)
XLA Ops:
  0.6 0.0 copy-start
  0.6 1.4 %copy-done = bf16[2,2,3,256,256]{4,3,2,1,0:T(8,128)(2,1)S(1)} copy-done((bf16[2,2,3,256,256]{4,3,2,1,0:T(8,128)(2,1)S(1)}, bf16[2,2,3,256,256]{4,3,2,1,0:T(8,128)(2,1)}, u32[]{:S(2)}) %copy-start) | copy-done | bytes 1572888
  2.0 0.0 copy-start.1
  2.0 1.0 %copy-done.1 = f32[2,3,128,128]{3,2,1,0:T(8,128)S(1)} copy-done((f32[2,3,128,128]{3,2,1,0:T(8,128)S(1)}, f32[2,3,128,128]{3,2,1,0:T(8,128)}, u32[]{:S(2)}) %copy-start.1) | copy-done | bytes 393240
  3.0 0.0 copy-start.2
  3.0 0.9 %copy-done.2 = f32[1,256,256]{2,1,0:T(8,128)S(1)} copy-done((f32[1,256,256]{2,1,0:T(8,128)S(1)}, f32[1,256,256]{2,1,0:T(8,128)}, u32[]{:S(2)}) %copy-start.2) | copy-done | bytes 262168
  4.0 0.0 copy-start.3
  4.0 0.9 %copy-done.3 = s32[1,256,256]{2,1,0:T(8,128)S(1)} copy-done((s32[1,256,256]{2,1,0:T(8,128)S(1)}, s32[1,256,256]{2,1,0:T(8,128)}, u32[]{:S(2)}) %copy-start.3) | copy-done | bytes 262168
  4.9 0.0 copy-start.4
  4.9 0.7 copy-done.4
  5.6 0.0 copy-start.5
  5.6 0.7 copy-done.5
  6.3 85.1 %shard_map.77 = (f32[1,256,256]{2,1,0:T(8,128)S(1)}, f32[1,256,256]{2,1,0:T(8,128)S(1)}) custom-call(f32[1,256,256]{2,1,0:T(8,128)S(1)} %copy-done.2, f32[2,3,128,128]{3,2,1,0:T(8,128)S(1)} %copy-done.1, s32[1,256,256]{2,1,0:T(8,128)S(1)} %copy-done.3, bf16[2,2,3,256,256]{4,3,2,1,0:T(8,128)(2,1)S(1)} %copy-done, f32[3]{0:T(128)S(1)} %copy-done.4, ...), custom_call_target="tpu_custom_call" | custom-call | tf_op jit(solution)/shard_map/pallas_call | solution.py:468
  91.4 0.7 copy.10
  92.1 0.7 copy.11
Async XLA Ops:
  0.6 1.4 %copy-start = (bf16[2,2,3,256,256]{4,3,2,1,0:T(8,128)(2,1)S(1)}, bf16[2,2,3,256,256]{4,3,2,1,0:T(8,128)(2,1)}, u32[]{:S(2)}) copy-start(bf16[2,2,3,256,256]{4,3,2,1,0:T(8,128)(2,1)} %constant.2.clone.tab) | copy-start | bytes 4718596
  2.0 1.0 %copy-start.1 = (f32[2,3,128,128]{3,2,1,0:T(8,128)S(1)}, f32[2,3,128,128]{3,2,1,0:T(8,128)}, u32[]{:S(2)}) copy-start(f32[2,3,128,128]{3,2,1,0:T(8,128)} %kernels.1) | copy-start | bytes 1179652
  3.0 0.9 %copy-start.2 = (f32[1,256,256]{2,1,0:T(8,128)S(1)}, f32[1,256,256]{2,1,0:T(8,128)}, u32[]{:S(2)}) copy-start(f32[1,256,256]{2,1,0:T(8,128)} %mask.1) | copy-start | bytes 786436
  4.0 0.9 %copy-start.3 = (s32[1,256,256]{2,1,0:T(8,128)S(1)}, s32[1,256,256]{2,1,0:T(8,128)}, u32[]{:S(2)}) copy-start(s32[1,256,256]{2,1,0:T(8,128)} %target.1) | copy-start | bytes 786436
  4.9 0.7 copy-start.4
  5.6 0.7 copy-start.5
where the time goes:
time: 93.8 us; the launch traced here: 92.8 us
  Pallas kernels  85.1 us (91%)
  local copies, waits for them, and re-layouts  7.01 us (7%)
    pallas_call x1, Pallas kernels, body(): pl.pallas_call(body_kernel, out_shape=(out, out), in_specs=[vmem, vmem, v...  85.1 us
    unnamed x14, local copies, waits for them, and re-layouts  7.01 us

commit v1 on v0

v1 whole, which is shorter than its diff:
```python
import functools
import math

import jax
import jax.numpy as jnp
import ml_dtypes
import numpy as np
from jax import lax
from jax.experimental import pallas as pl
from jax.experimental.pallas import tpu as pltpu
from jax.sharding import PartitionSpec as P

GRID_W = 8
STEEP = 20.0
THRESH = 0.33
BLK = 128
EXTENT = 3 * BLK
CORE = 2 * BLK
HALO = BLK // 2
HALF_SQRT3 = math.sqrt(3.0) / 2.0
MESH = pl.DeviceIdType.MESH
F32 = jnp.float32
BF16 = jnp.bfloat16


def dft_tables():
    place = np.arange(BLK)
    groups = (3 * place, 3 * place + 1, -(3 * place + 1))
    mats = []
    for freq in groups:
        angle = 2.0 * np.pi * (np.outer(place, freq) % EXTENT) / EXTENT
        c, s = np.cos(angle), -np.sin(angle)
        mats.append(np.block([[c, s], [-s, c]]))
    fwd = np.stack(mats).astype(np.float32)
    both = np.stack([fwd, fwd.transpose(0, 2, 1)])
    high = both.astype(ml_dtypes.bfloat16)
    low = (both - high.astype(np.float32)).astype(ml_dtypes.bfloat16)
    return np.stack([high, low])


def split(x):
    high = x.astype(BF16)
    return high, (x - high.astype(F32)).astype(BF16)


def dot(a, b):
    return jnp.dot(a, b, preferred_element_type=F32)


def mul_right(x, high, low):
    xh, xl = split(x)
    return dot(xh, high) + (dot(xh, low) + dot(xl, high))


def mul_left(high, low, x):
    xh, xl = split(x)
    return dot(high, xh) + (dot(low, xh) + dot(high, xl))


def fwd_mat(tab, g):
    return tab[0, 0, g], tab[1, 0, g]


def t_mat(tab, g):
    return tab[0, 1, g], tab[1, 1, g]


def lanes(re, im):
    return jnp.concatenate([re, im], axis=1)


def rows(re, im):
    return jnp.concatenate([re, im], axis=0)


def response_rows(kernels, tab, mid):
    scale = 1.0 / (EXTENT * EXTENT)
    re = jnp.concatenate([kernels[0, k] for k in range(3)], axis=1) * scale
    im = jnp.concatenate([kernels[1, k] for k in range(3)], axis=1) * -scale
    taps = rows(re, im)
    for g in range(3):
        out = mul_left(*t_mat(tab, g), taps)
        mid[0, pl.ds(g * BLK, BLK), :] = out[:BLK]
        mid[1, pl.ds(g * BLK, BLK), :] = out[BLK:]


def response_cols(k, tab, mid, resp):
    cols = pl.ds(k * BLK, BLK)
    x = lanes(mid[0, :, cols], mid[1, :, cols])
    for g in range(3):
        out = mul_right(x, *fwd_mat(tab, g))
        resp[0, :, pl.ds(k * EXTENT + g * BLK, BLK)] = out[:, :BLK]
        resp[1, :, pl.ds(k * EXTENT + g * BLK, BLK)] = out[:, BLK:]


def spectrum_cols(ext, places, tab, mid):
    x0, x1, x2 = (
        jnp.concatenate([ext[pl.ds(s, n), pl.ds(j * BLK, BLK)] for s, n in places], axis=0) for j in range(3)
    )
    z0 = x0 + x1 + x2
    z1 = lanes(x0 - 0.5 * (x1 + x2), HALF_SQRT3 * (x2 - x1))
    h0, l0 = fwd_mat(tab, 0)
    outs = (mul_right(z0, h0[:BLK], l0[:BLK]), mul_right(z1, *fwd_mat(tab, 1)))
    for g, out in enumerate(outs):
        at = 0
        for s, n in places:
            mid[0, pl.ds(s, n), pl.ds(g * BLK, BLK)] = out[at : at + n, :BLK]
            mid[1, pl.ds(s, n), pl.ds(g * BLK, BLK)] = out[at : at + n, BLK:]
            at += n


def spectrum_rows(tab, mid, spec):
    two = pl.ds(0, CORE)
    a_re, b_re, c_re = (mid[0, pl.ds(j * BLK, BLK), two] for j in range(3))
    a_im, b_im, c_im = (mid[1, pl.ds(j * BLK, BLK), two] for j in range(3))
    s_re, s_im = b_re + c_re, b_im + c_im
    e_re, e_im = a_re - 0.5 * s_re, a_im - 0.5 * s_im
    f_re, f_im = HALF_SQRT3 * (b_re - c_re), HALF_SQRT3 * (b_im - c_im)
    z_re, z_im = a_re + s_re, a_im + s_im
    z_re = lanes(z_re, z_re[:, BLK:])
    z_im = lanes(z_im, -z_im[:, BLK:])
    out = mul_left(*t_mat(tab, 0), rows(z_re, z_im))
    spec[0, pl.ds(0, BLK), :] = out[:BLK]
    spec[1, pl.ds(0, BLK), :] = out[BLK:]
    out1 = mul_left(*t_mat(tab, 1), rows(e_re + f_im, e_im - f_re))
    out2 = mul_left(*t_mat(tab, 2), rows(e_re - f_im, e_im + f_re))
    spec[0, pl.ds(BLK, BLK), :] = lanes(out1[:BLK], out2[:BLK, BLK:])
    spec[1, pl.ds(BLK, BLK), :] = lanes(out1[BLK:], -out2[BLK:, BLK:])
    spec[0, pl.ds(2 * BLK, BLK), :] = lanes(out2[:BLK], out1[:BLK, BLK:])
    spec[1, pl.ds(2 * BLK, BLK), :] = lanes(out2[BLK:], -out1[BLK:, BLK:])


PAIRS = [[(b // 3, b % 3) for b in range(s, min(s + 2, 9))] for s in range(0, 9, 2)]


def field_rows(pair, resp, spec, tab, mid):
    width = len(pair) * BLK
    start = (pair[0][0] * 3 + pair[0][1]) * BLK
    cols = pl.ds(start, width)
    t = []
    for g in range(3):
        block = pl.ds(g * BLK, BLK)
        q_re, q_im = resp[0, block, cols], resp[1, block, cols]
        e_re = jnp.concatenate([spec[0, block, pl.ds(f * BLK, BLK)] for _, f in pair], axis=1)
        e_im = jnp.concatenate([spec[1, block, pl.ds(f * BLK, BLK)] for _, f in pair], axis=1)
        x = rows(e_re * q_re + e_im * q_im, e_im * q_re - e_re * q_im)
        t.append(mul_left(*fwd_mat(tab, g), x))
    s, d = t[1] + t[2], HALF_SQRT3 * (t[1] - t[2])
    first, e = t[0] + s, t[0] - 0.5 * s
    upper, lower = pl.ds(0, BLK), pl.ds(BLK, BLK)
    mid[0, upper, cols] = first[:BLK]
    mid[1, upper, cols] = first[BLK:]
    mid[0, lower, cols] = e[:BLK] - d[BLK:]
    mid[1, lower, cols] = e[BLK:] + d[:BLK]


def field_cols(h, tab, mid, field):
    t = []
    for g in range(3):
        x = jnp.concatenate(
            [
                lanes(*(mid[c, pl.ds(h * BLK, BLK), pl.ds(k * EXTENT + g * BLK, BLK)] for c in range(2)))
                for k in range(3)
            ],
            axis=0,
        )
        t.append(mul_right(x, *t_mat(tab, g)))
    s, d = t[1] + t[2], HALF_SQRT3 * (t[1] - t[2])
    first, e = t[0] + s, t[0] - 0.5 * s
    field[h, 0] = lanes(first[:, :BLK], e[:, :BLK] - d[:, BLK:])
    field[h, 1] = lanes(first[:, BLK:], e[:, BLK:] + d[:, :BLK])


def source_cols(h, slope, weight, tab, field, mid):
    scaled = jnp.concatenate([weight[k] * slope for k in range(3)], axis=0)
    s_re, s_im = scaled * field[h, 0], scaled * field[h, 1]
    a_re, a_im, b_re, b_im = s_re[:, :BLK], s_im[:, :BLK], s_re[:, BLK:], s_im[:, BLK:]
    e_re, e_im = a_re - 0.5 * b_re, a_im - 0.5 * b_im
    f_re, f_im = HALF_SQRT3 * b_re, HALF_SQRT3 * b_im
    z = (
        lanes(a_re + b_re, a_im + b_im),
        lanes(e_re + f_im, e_im - f_re),
        lanes(e_re - f_im, e_im + f_re),
    )
    for g in range(3):
        out = mul_right(z[g], *fwd_mat(tab, g))
        for k in range(3):
            cols = pl.ds(k * EXTENT + g * BLK, BLK)
            mid[0, pl.ds(h * BLK, BLK), cols] = out[k * BLK : (k + 1) * BLK, :BLK]
            mid[1, pl.ds(h * BLK, BLK), cols] = out[k * BLK : (k + 1) * BLK, BLK:]


def source_rows(pair, resp, tab, mid, acc):
    width = len(pair) * BLK
    start = (pair[0][0] * 3 + pair[0][1]) * BLK
    cols = pl.ds(start, width)
    upper, lower = pl.ds(0, BLK), pl.ds(BLK, BLK)
    a_re, a_im, b_re, b_im = mid[0, upper, cols], mid[1, upper, cols], mid[0, lower, cols], mid[1, lower, cols]
    e_re, e_im = a_re - 0.5 * b_re, a_im - 0.5 * b_im
    f_re, f_im = HALF_SQRT3 * b_re, HALF_SQRT3 * b_im
    z = (
        rows(a_re + b_re, a_im + b_im),
        rows(e_re + f_im, e_im - f_re),
        rows(e_re - f_im, e_im + f_re),
    )
    for g in range(3):
        out = mul_left(*t_mat(tab, g), z[g])
        block = pl.ds(g * BLK, BLK)
        o_re, o_im = out[:BLK], out[BLK:]
        q_re, q_im = resp[0, block, cols], resp[1, block, cols]
        p_re, p_im = o_re * q_re - o_im * q_im, o_re * q_im + o_im * q_re
        for n, (k, f) in enumerate(pair):
            into = pl.ds(f * BLK, BLK)
            part = slice(n * BLK, (n + 1) * BLK)
            if k == 0:
                acc[0, block, into] = p_re[:, part]
                acc[1, block, into] = p_im[:, part]
            else:
                acc[0, block, into] += p_re[:, part]
                acc[1, block, into] += p_im[:, part]


def gradient_rows(acc, tab, mid):
    p0, p1, p2 = (pl.ds(g * BLK, BLK) for g in range(3))
    t0 = mul_left(*fwd_mat(tab, 0), rows(acc[0, p0, :], acc[1, p0, :]))
    t0_re, t0_im = t0[:BLK], t0[BLK:]
    t0_re = lanes(t0_re[:, :BLK], t0_re[:, BLK:CORE] + t0_re[:, CORE:])
    t0_im = lanes(t0_im[:, :BLK], t0_im[:, BLK:CORE] - t0_im[:, CORE:])
    x_re = lanes(acc[0, p1, p0], acc[0, p1, p1] + acc[0, p2, p2])
    x_im = lanes(acc[1, p1, p0], acc[1, p1, p1] - acc[1, p2, p2])
    t1 = mul_left(*fwd_mat(tab, 1), rows(x_re, x_im))
    x_re = lanes(acc[0, p2, p0], acc[0, p2, p1] + acc[0, p1, p2])
    x_im = lanes(acc[1, p2, p0], acc[1, p2, p1] - acc[1, p1, p2])
    t2 = mul_left(*fwd_mat(tab, 2), rows(x_re, x_im))
    s, d = t1 + t2, HALF_SQRT3 * (t1 - t2)
    e_re, e_im = t0_re - 0.5 * s[:BLK], t0_im - 0.5 * s[BLK:]
    two = pl.ds(0, CORE)
    mid[0, p0, two], mid[1, p0, two] = t0_re + s[:BLK], t0_im + s[BLK:]
    mid[0, p1, two], mid[1, p1, two] = e_re - d[BLK:], e_im + d[:BLK]
    mid[0, p2, two], mid[1, p2, two] = e_re + d[BLK:], e_im - d[:BLK]


def gradient_cols(places, tab, mid):
    h0, l0 = t_mat(tab, 0)
    part = lambda c, g: jnp.concatenate([mid[c, pl.ds(s, n), pl.ds(g * BLK, BLK)] for s, n in places], axis=0)
    r0 = mul_right(lanes(part(0, 0), part(1, 0)), h0[:, :BLK], l0[:, :BLK])
    r1 = mul_right(lanes(part(0, 1), part(1, 1)), *t_mat(tab, 1))
    e, d = r0 - 0.5 * r1[:, :BLK], HALF_SQRT3 * r1[:, BLK:]
    return r0 + r1[:, :BLK], e - d, e + d


QUARTER = CORE // 4
EIGHTH = CORE // 8
PART = HALO // 4


def body_kernel(
    mask_hbm, kernels_hbm, target_hbm, tab_hbm, weight, link, resist_out, grad_out,
    mask, kernels, target, tab, mid, wide, resp, spec, field, acc, ext, resist,
    side_out, side_in, vert_out, vert_in, corner_out, corner_in, margin,
    clear_in, clear_sum, clear_far, power, power_in, power_mine, power_far, power_all,
    halo_parts, halo_in, core_parts, core_in, fold_out, fold_in, bend_out, bend_in, edge_out, edge_in,
    mine, other, gathered,
    load_sem, store_sem, side_send, side_recv, vert_send, vert_recv, corner_send, corner_recv, share_send, share_recv,
    clear_send, clear_recv, cfar_send, cfar_recv,
    psc_send, psc_recv, pfar_send, pfar_recv, pall_send, pall_recv,
    hsc_send, hsc_recv, gsc_send, gsc_recv, fold_send, fold_recv, bend_send, bend_recv,
    edge_send, edge_recv, gfar_send, gfar_recv, all_send, all_recv,
):
    tile = lax.axis_index("tile")
    kern = lax.axis_index("kern")
    tiles = lax.axis_size("tile")
    x = kern // 2
    half = kern % 2
    column = (tile + GRID_W // 2) % GRID_W
    right_ok = jnp.where((column < GRID_W - 1) & (tile + 1 < tiles), 1.0, 0.0)
    down_ok = jnp.where(tile + GRID_W < tiles, 1.0, 0.0)
    right_link = link[0, 0].astype(F32) * right_ok
    down_link = link[0, 1].astype(F32) * down_ok

    def at(tile_by, kern_index):
        return {"tile": (tile + tile_by + tiles) % tiles, "kern": kern_index}

    right, left = at(1, kern), at(-1, kern)
    far = at(0, 2 * x + 1 - half)
    x_at = [(x + d) % 4 for d in range(4)]
    peers = [at(0, 2 * x_at[d] + half) for d in range(4)]
    verticals = [at(s * GRID_W + e, kern) for s in (1, -1) for e in (-1, 0, 1)]
    sign = 2 * (x % 2) - 1
    crossed = 2 * (x + 1 - 2 * (x % 2)) + half
    crosses = [at(sign * GRID_W + e, crossed) for e in (-1, 0, 1)]

    barrier = pltpu.get_barrier_semaphore()
    partners = verticals + [right, left, far] + peers[1:] + crosses
    for one in partners:
        pl.semaphore_signal(barrier, inc=1, device_id=one, device_id_type=MESH)

    loads = [
        pltpu.make_async_copy(src, dst, load_sem.at[n])
        for n, (src, dst) in enumerate(((mask_hbm, mask), (kernels_hbm, kernels), (tab_hbm, tab), (target_hbm, target)))
    ]
    for copy in loads:
        copy.start()
    started = []

    def remote(src, dst, send, recv, device):
        copy = pltpu.make_async_remote_copy(
            src_ref=src, dst_ref=dst, send_sem=send, recv_sem=recv, device_id=device, device_id_type=MESH
        )
        copy.start()
        started.append(copy)
        return copy

    lane = lax.broadcasted_iota(jnp.int32, (BLK, BLK), 1) < HALO
    lane_all = lax.broadcasted_iota(jnp.int32, (CORE, BLK), 1) < HALO
    lane_part = lax.broadcasted_iota(jnp.int32, (PART, BLK), 1) < HALO

    loads[0].wait()
    a0, a1 = mask[0, :, pl.ds(0, BLK)], mask[0, :, pl.ds(BLK, BLK)]
    r0, r1 = pltpu.roll(a0, HALO, 1), pltpu.roll(a1, HALO, 1)
    outer = jnp.where(lane_all, r1, r0)
    inner = jnp.where(lane_all, r0, r1)
    flipped = pltpu.roll(outer, HALO, 1)
    side_out[0] = jnp.where(lane, outer[:BLK], flipped[BLK:]) * right_link
    side_out[1] = jnp.where(lane, flipped[:BLK], outer[BLK:])
    middle = pl.ds(HALO, CORE)
    ext[middle, pl.ds(BLK, BLK)] = inner
    ext[middle, pl.ds(0, BLK)] = outer
    for n, first in enumerate((CORE - HALO, 0)):
        block = pl.ds(pl.multiple_of(HALO + first + PART * x, PART), PART)
        outer_part = ext[block, pl.ds(0, BLK)]
        vert_out[n, pl.ds(0, PART), pl.ds(0, BLK)] = outer_part
        vert_out[n, pl.ds(0, PART), pl.ds(BLK, BLK)] = ext[block, pl.ds(BLK, BLK)]
        vert_out[n, pl.ds(PART, 8), pl.ds(0, BLK)] = jnp.full((8, BLK), down_link, F32)
        vert_out[n, pl.ds(PART, 8), pl.ds(BLK, BLK)] = jnp.full((8, BLK), right_link, F32)
        corner_out[n, 0] = outer_part
        corner_out[n, 1] = outer_part * right_link

    pl.semaphore_wait(barrier, len(partners))
    verts = [
        remote(vert_out.at[0], vert_in.at[0], vert_send.at[0], vert_recv.at[0], verticals[1]),
        remote(vert_out.at[1], vert_in.at[1], vert_send.at[1], vert_recv.at[1], verticals[4]),
        remote(corner_out.at[0, 1], corner_in.at[0], corner_send.at[0], corner_recv.at[0], verticals[2]),
        remote(corner_out.at[0, 0], corner_in.at[1], corner_send.at[1], corner_recv.at[1], verticals[0]),
        remote(corner_out.at[1, 1], corner_in.at[2], corner_send.at[2], corner_recv.at[2], verticals[5]),
        remote(corner_out.at[1, 0], corner_in.at[3], corner_send.at[3], corner_recv.at[3], verticals[3]),
    ]
    sides = [
        remote(side_out.at[0], side_in.at[0], side_send.at[0], side_recv.at[0], right),
        remote(side_out.at[1], side_in.at[1], side_send.at[1], side_recv.at[1], left),
    ]

    loads[1].wait()
    taps = [[jnp.sum(kernels[c, k], keepdims=True) for k in range(3)] for c in range(2)]
    clear_part = sum(weight[k] * (taps[0][k] * taps[0][k] + taps[1][k] * taps[1][k]) for k in range(3))
    clear_in[x] = jnp.broadcast_to(clear_part, (8, BLK))
    clears = [
        remote(clear_in.at[x], clear_in.at[x], clear_send.at[d - 1], clear_recv.at[d - 1], peers[d])
        for d in range(1, 4)
    ]
    loads[2].wait()
    response_rows(kernels, tab, mid)
    response_cols(0, tab, mid, resp)

    for copy in sides:
        copy.wait_recv()
    from_left, from_right = side_in[0], side_in[1] * right_link
    upper, lower = pl.ds(HALO, BLK), pl.ds(HALO + BLK, BLK)
    up_outer, low_outer = ext[upper, pl.ds(0, BLK)], ext[lower, pl.ds(0, BLK)]
    ext[upper, pl.ds(0, BLK)] = jnp.where(lane, from_left, up_outer)
    ext[lower, pl.ds(0, BLK)] = jnp.where(lane, pltpu.roll(from_left, HALO, 1), low_outer)
    ext[upper, pl.ds(CORE, BLK)] = jnp.where(lane, up_outer, pltpu.roll(from_right, HALO, 1))
    ext[lower, pl.ds(CORE, BLK)] = jnp.where(lane, low_outer, from_right)

    for copy in verts:
        copy.wait_recv()
    down_above, right_above = vert_in[0, pl.ds(PART, 1), pl.ds(0, 1)], vert_in[0, pl.ds(PART, 1), pl.ds(BLK, 1)]
    right_below = vert_in[1, pl.ds(PART, 1), pl.ds(BLK, 1)]
    for n, (factor, beside) in enumerate(((down_above, right_above), (down_link, right_below))):
        edge = vert_in[n, pl.ds(0, PART), pl.ds(0, BLK)]
        margin[x, n, :, pl.ds(0, BLK)] = jnp.where(lane_part, corner_in[2 * n], edge) * factor
        margin[x, n, :, pl.ds(BLK, BLK)] = vert_in[n, pl.ds(0, PART), pl.ds(BLK, BLK)] * factor
        margin[x, n, :, pl.ds(CORE, BLK)] = jnp.where(lane_part, edge, corner_in[2 * n + 1] * beside) * factor
    shares = [
        remote(margin.at[x], margin.at[x], share_send.at[d - 1], share_recv.at[d - 1], peers[d])
        for d in range(1, 4)
    ]
    for copy in clears:
        copy.wait_recv()
    clear_sum[...] = clear_in[0] + clear_in[1] + clear_in[2] + clear_in[3]
    clear_copy = remote(clear_sum, clear_far, cfar_send, cfar_recv, far)
    response_cols(1, tab, mid, resp)
    response_cols(2, tab, mid, resp)
    spectrum_cols(ext, [(HALO, CORE)], tab, mid)
    for copy in shares:
        copy.wait_recv()
    for q in range(4):
        ext[pl.ds(PART * q, PART), :] = margin[q, 0]
        ext[pl.ds(HALO + CORE + PART * q, PART), :] = margin[q, 1]
    spectrum_cols(ext, [(0, HALO), (HALO + CORE, HALO)], tab, mid)
    spectrum_rows(tab, mid, spec)
    for pair in PAIRS:
        field_rows(pair, resp, spec, tab, wide)

    scatter = []
    for h in range(2):
        field_cols(h, tab, wide, field)
        for q in range(4):
            p = 0.0
            for k in range(3):
                block = pl.ds(k * BLK + q * EIGHTH, EIGHTH)
                f_re, f_im = field[h, 0, block, :], field[h, 1, block, :]
                p = p + weight[k] * (f_re * f_re + f_im * f_im)
            power[h, q] = p
        scatter.append([
            remote(power.at[h, x_at[d]], power_in.at[h, d - 1], psc_send.at[h, d - 1], psc_recv.at[h, d - 1], peers[d])
            for d in range(1, 4)
        ])
    loads[3].wait()
    clear_copy.wait_recv()
    swaps = []
    for h in range(2):
        for copy in scatter[h]:
            copy.wait_recv()
        power_mine[h] = power[h, x] + power_in[h, 0] + power_in[h, 1] + power_in[h, 2]
        swaps.append(remote(power_mine.at[h], power_far.at[h], pfar_send.at[h], pfar_recv.at[h], far))
    gathers = []
    for h in range(2):
        swaps[h].wait_recv()
        power_all[h, x] = power_mine[h] + power_far[h]
        gathers.append([
            remote(power_all.at[h, x], power_all.at[h, x], pall_send.at[h, d - 1], pall_recv.at[h, d - 1], peers[d])
            for d in range(1, 4)
        ])
    clear = (clear_sum[...] + clear_far[...])[0:1, 0:1]
    for h in range(2):
        for copy in gathers[h]:
            copy.wait_recv()
        total = jnp.concatenate([power_all[h, q] for q in range(4)], axis=0)
        printed = 1.0 / (1.0 + jnp.exp(-STEEP * (total / clear - THRESH)))
        block = pl.ds(h * BLK, BLK)
        resist[0, block, :] = printed
        wanted = target[0, block, :].astype(F32)
        slope = (4.0 * STEEP) * (printed - wanted) * printed * (1.0 - printed) / clear
        source_cols(h, slope, weight, tab, field, wide)
    store = pltpu.make_async_copy(resist, resist_out, store_sem.at[0])
    store.start()
    for pair in PAIRS:
        source_rows(pair, resp, tab, wide, acc)
    gradient_rows(acc, tab, mid)

    blocks = gradient_cols([(0, HALO), (HALO + CORE, HALO)], tab, mid)
    for c in range(3):
        for q, start in enumerate((64, 96, 32, 0)):
            halo_parts[q, :, pl.ds(c * BLK, BLK)] = blocks[c][start : start + 32]
    halo_scatter = [
        remote(halo_parts.at[x_at[d]], halo_in.at[d - 1], hsc_send.at[d - 1], hsc_recv.at[d - 1], peers[d])
        for d in range(1, 4)
    ]
    blocks = gradient_cols([(HALO, CORE)], tab, mid)
    for c in range(3):
        for q in range(4):
            core_parts[q, :, pl.ds(c * BLK, BLK)] = blocks[c][q * QUARTER : (q + 1) * QUARTER]
    core_scatter = [
        remote(core_parts.at[x_at[d]], core_in.at[d - 1], gsc_send.at[d - 1], gsc_recv.at[d - 1], peers[d])
        for d in range(1, 4)
    ]

    low_x = x < 2
    for copy in halo_scatter:
        copy.wait_recv()
    is_low = jnp.where(low_x, 1.0, 0.0)
    down_factor = is_low * down_link + (1.0 - is_low) * down_above
    right_factor = is_low * right_below + (1.0 - is_low) * right_above
    fold_out[...] = (halo_parts[x] + halo_in[0] + halo_in[1] + halo_in[2]) * down_factor
    bend_out[0] = fold_out[:, pl.ds(0, BLK)]
    bend_out[1] = fold_out[:, pl.ds(CORE, BLK)] * right_factor
    slot = jnp.where((x == 1) | (x == 2), 1, 0)
    step = jnp.where(low_x, GRID_W, -GRID_W)
    owner = jnp.where(low_x, 0, 6) + half
    folds = [
        remote(fold_out, fold_in.at[slot], fold_send, fold_recv.at[slot], at(step, owner)),
        remote(bend_out.at[0], bend_in.at[slot, 0], bend_send.at[0], bend_recv.at[slot, 0], at(step - 1, owner)),
        remote(bend_out.at[1], bend_in.at[slot, 1], bend_send.at[1], bend_recv.at[slot, 1], at(step + 1, owner)),
    ]

    for copy in core_scatter:
        copy.wait_recv()
    owned = core_parts[x] + core_in[0] + core_in[1] + core_in[2]
    edge_out[0] = owned[:, CORE:] * right_link
    edge_out[1] = owned[:, :BLK]
    edges = [
        remote(edge_out.at[0], edge_in.at[0], edge_send.at[0], edge_recv.at[0], right),
        remote(edge_out.at[1], edge_in.at[1], edge_send.at[1], edge_recv.at[1], left),
    ]
    core_parts[x] = owned

    @pl.when((x == 0) | (x == 3))
    def _():
        for s in range(2):
            waits = [
                (fold_out, fold_in.at[s], fold_send, fold_recv.at[s]),
                (bend_out.at[0], bend_in.at[s, 0], bend_send.at[0], bend_recv.at[s, 0]),
                (bend_out.at[1], bend_in.at[s, 1], bend_send.at[1], bend_recv.at[s, 1]),
            ]
            for src, dst, send, recv in waits:
                pltpu.make_async_remote_copy(
                    src_ref=src, dst_ref=dst, send_sem=send, recv_sem=recv, device_id=far, device_id_type=MESH
                ).wait_recv()
            block = pl.ds(32 * s, 32)
            core_parts[x, block, pl.ds(0, BLK)] += fold_in[s, :, pl.ds(0, BLK)] + bend_in[s, 1]
            core_parts[x, block, pl.ds(BLK, BLK)] += fold_in[s, :, pl.ds(BLK, BLK)]
            core_parts[x, block, pl.ds(CORE, BLK)] += fold_in[s, :, pl.ds(CORE, BLK)] + bend_in[s, 0] * right_link

    for copy in edges:
        copy.wait_recv()
    near_lane = lax.broadcasted_iota(jnp.int32, (QUARTER, BLK), 1) < HALO
    b0 = core_parts[x, :, pl.ds(0, BLK)] + edge_in[0]
    b1 = core_parts[x, :, pl.ds(BLK, BLK)]
    b2 = core_parts[x, :, pl.ds(CORE, BLK)] + edge_in[1] * right_link
    c0, c1, c2 = (pltpu.roll(b, HALO, 1) for b in (b0, b1, b2))
    whole = lanes(jnp.where(near_lane, c0, c1), jnp.where(near_lane, c1, c2))
    swaps = []
    for h in range(2):
        mine[h] = whole[h * 32 : (h + 1) * 32]
        swaps.append(remote(mine.at[h], other.at[h], gfar_send.at[h], gfar_recv.at[h], far))
    finals = []
    for h in range(2):
        swaps[h].wait_recv()
        gathered[x, h] = mine[h] + other[h]
        finals.append([
            remote(gathered.at[x, h], gathered.at[x, h], all_send.at[h, d - 1], all_recv.at[h, d - 1], peers[d])
            for d in range(1, 4)
        ])
    for h in range(2):
        for copy in finals[h]:
            copy.wait_recv()
    stores = []
    for q in range(4):
        for h in range(2):
            stores.append(
                pltpu.make_async_copy(
                    gathered.at[q, h], grad_out.at[0, pl.ds(64 * q + 32 * h, 32)], store_sem.at[1 + 2 * q + h]
                )
            )
            stores[-1].start()
    for copy in started:
        copy.wait_send()
    store.wait()
    for copy in stores:
        copy.wait()


def body(mask, kernels, weight, link, target):
    smem = pl.BlockSpec(memory_space=pltpu.SMEM)
    anywhere = pl.BlockSpec(memory_space=pl.ANY)
    dma = pltpu.SemaphoreType.DMA
    f32 = lambda *shape: pltpu.VMEM(shape, F32)
    buffers = [
        f32(1, CORE, CORE), f32(2, 3, BLK, BLK), pltpu.VMEM((1, CORE, CORE), jnp.int32),
        pltpu.VMEM((2, 2, 3, CORE, CORE), BF16),
        f32(2, EXTENT, EXTENT), f32(2, CORE, 3 * EXTENT), f32(2, EXTENT, 3 * EXTENT), f32(2, EXTENT, EXTENT),
        f32(2, 2, EXTENT, CORE), f32(2, EXTENT, EXTENT), f32(EXTENT, EXTENT), f32(1, CORE, CORE),
        f32(2, BLK, BLK), f32(2, BLK, BLK), f32(2, PART + 8, CORE), f32(2, PART + 8, CORE),
        f32(2, 2, PART, BLK), f32(4, PART, BLK), f32(4, 2, PART, EXTENT),
        f32(4, 8, BLK), f32(8, BLK), f32(8, BLK),
        f32(2, 4, EIGHTH, CORE), f32(2, 3, EIGHTH, CORE), f32(2, EIGHTH, CORE), f32(2, EIGHTH, CORE),
        f32(2, 4, EIGHTH, CORE),
        f32(4, 32, EXTENT), f32(3, 32, EXTENT), f32(4, QUARTER, EXTENT), f32(3, QUARTER, EXTENT),
        f32(32, EXTENT), f32(2, 32, EXTENT), f32(2, 32, BLK), f32(2, 2, 32, BLK),
        f32(2, QUARTER, BLK), f32(2, QUARTER, BLK),
        f32(2, 32, CORE), f32(2, 32, CORE), f32(4, 2, 32, CORE),
    ]
    sems = [dma((4,)), dma((9,))] + [dma((2,))] * 4 + [dma((4,))] * 2 + [dma((3,))] * 2
    sems += [dma((3,))] * 2 + [dma] * 2
    sems += [dma((2, 3))] * 2 + [dma((2,))] * 2 + [dma((2, 3))] * 2
    sems += [dma((3,))] * 4 + [dma, dma((2,)), dma((2,)), dma((2, 2))]
    sems += [dma((2,))] * 4 + [dma((2, 3))] * 2
    out = jax.ShapeDtypeStruct((1, CORE, CORE), F32)
    return pl.pallas_call(
        body_kernel,
        out_shape=(out, out),
        in_specs=[anywhere] * 4 + [smem] * 2,
        out_specs=(anywhere, anywhere),
        scratch_shapes=buffers + sems,
        compiler_params=pltpu.CompilerParams(
            collective_id=0, has_side_effects=True, vmem_limit_bytes=60 * 2**20
        ),
    )(mask, kernels, target, jnp.asarray(dft_tables()), weight, link)


def solution(mesh):
    in_specs = (
        P("tile", None, None),
        P(None, "kern", None, None),
        P("kern"),
        P("tile", None),
        P("tile", None, None),
    )
    out_specs = (P("tile", None, None), P("tile", None, None))
    return jax.shard_map(body, mesh=mesh, in_specs=in_specs, out_specs=out_specs, check_vma=False)
```

time: 93.8 us -> 73.8 us (0.79)
  Pallas kernels: 85.1 us -> 69.6 us
  local copies, waits for them, and re-layouts: 7.01 us -> 3.34 us
    pallas_call x1, Pallas kernels: 85.1 us -> 69.6 us  [body(): pl.pallas_call(body_kernel, out_shape=(out, out), in_specs=[anywhere] * 4...]
    unnamed x14 -> x2, local copies, waits for them, and re-layouts: 7.01 us -> 3.34 us
where the time goes in v1:
time: 73.8 us; the launch traced here: 73.6 us
  Pallas kernels  69.6 us (94%)
  local copies, waits for them, and re-layouts  3.34 us (5%)
    pallas_call x1, Pallas kernels, body(): pl.pallas_call(body_kernel, out_shape=(out, out), in_specs=[anywhere] * 4...  69.6 us
    unnamed x2, local copies, waits for them, and re-layouts  3.34 us

profile of v1, /device:TPU:1, one launch (start us, length us, event | category | flops | bytes accessed | tf_op | source)
XLA Modules:
  0.0 73.6 jit_solution(4822097947492116103)
XLA Ops:
  0.6 69.6 %shard_map.77 = (f32[1,256,256]{2,1,0:T(8,128)}, f32[1,256,256]{2,1,0:T(8,128)}) custom-call(f32[1,256,256]{2,1,0:T(8,128)} %mask_hbm.1, f32[2,3,128,128]{3,2,1,0:T(8,128)} %kernels_hbm.1, s32[1,256,256]{2,1,0:T(8,128)} %target_hbm.1, bf16[2,2,3,256,256]{4,3,2,1,0:T(8,128)(2,1)} %constant.2.clone.tab_hbm, f32[3]{0:T(128)} %weight.1, s32[1,2]{1,0:T(1,128)} %link.1), custom_call_target="tpu_custom_call" | custom-call | tf_op jit(solution)/shard_map/pallas_call | solution.py:580
  70.2 1.7 %copy.10 = f32[1,256,256]{2,1,0:T(8,128)} copy(f32[1,256,256]{2,1,0:T(8,128)} %get-tuple-element.4) | data formatting | bytes 524288
  71.9 1.7 %copy.11 = f32[1,256,256]{2,1,0:T(8,128)} copy(f32[1,256,256]{2,1,0:T(8,128)} %get-tuple-element.5) | data formatting | bytes 524288

commit v2 on v1

--- a/solution.py
+++ b/solution.py
@@ -254,14 +254,42 @@
 PART = HALO // 4
 
 
+def low_lanes(n):
+    return lax.broadcasted_iota(jnp.int32, (n, BLK), 1) < HALO
+
+
+def pack_low(x):
+    n = x.shape[0] // 2
+    return jnp.where(low_lanes(n), x[:n], pltpu.roll(x[n:], HALO, 1))
+
+
+def pack_high(x):
+    n = x.shape[0] // 2
+    return jnp.where(low_lanes(n), pltpu.roll(x[:n], HALO, 1), x[n:])
+
+
+def unpack_low(x):
+    return rows(x, pltpu.roll(x, HALO, 1))
+
+
+def unpack_high(x):
+    return rows(pltpu.roll(x, HALO, 1), x)
+
+
+def core_blocks(x):
+    c0, c1, c2 = (pltpu.roll(x[:, j * BLK : (j + 1) * BLK], HALO, 1) for j in range(3))
+    low = low_lanes(x.shape[0])
+    return c0, c2, lanes(jnp.where(low, c0, c1), jnp.where(low, c1, c2))
+
+
 def body_kernel(
-    mask_hbm, kernels_hbm, target_hbm, tab_hbm, weight, link, resist_out, grad_out,
+    mask_hbm, kernels_hbm, target_hbm, tab_hbm, weight_hbm, link_hbm, out,
     mask, kernels, target, tab, mid, wide, resp, spec, field, acc, ext, resist,
     side_out, side_in, vert_out, vert_in, corner_out, corner_in, margin,
     clear_in, clear_sum, clear_far, power, power_in, power_mine, power_far, power_all,
-    halo_parts, halo_in, core_parts, core_in, fold_out, fold_in, bend_out, bend_in, edge_out, edge_in,
+    halo_parts, halo_in, core_parts, core_in, fold_out, fold_in, bend_out, bend_in, edge_out, edge_in, whole,
     mine, other, gathered,
-    load_sem, store_sem, side_send, side_recv, vert_send, vert_recv, corner_send, corner_recv, share_send, share_recv,
+    weight, link, load_sem, store_sem, side_send, side_recv, vert_send, vert_recv, corner_send, corner_recv, share_send, share_recv,
     clear_send, clear_recv, cfar_send, cfar_recv,
     psc_send, psc_recv, pfar_send, pfar_recv, pall_send, pall_recv,
     hsc_send, hsc_recv, gsc_send, gsc_recv, fold_send, fold_recv, bend_send, bend_recv,
@@ -275,82 +303,114 @@
     column = (tile + GRID_W // 2) % GRID_W
     right_ok = jnp.where((column < GRID_W - 1) & (tile + 1 < tiles), 1.0, 0.0)
     down_ok = jnp.where(tile + GRID_W < tiles, 1.0, 0.0)
-    right_link = link[0, 0].astype(F32) * right_ok
-    down_link = link[0, 1].astype(F32) * down_ok
+
+    def valid(tile_by):
+        return (tile + tile_by >= 0) & (tile + tile_by < tiles)
 
     def at(tile_by, kern_index):
         return {"tile": (tile + tile_by + tiles) % tiles, "kern": kern_index}
 
-    right, left = at(1, kern), at(-1, kern)
     far = at(0, 2 * x + 1 - half)
     x_at = [(x + d) % 4 for d in range(4)]
     peers = [at(0, 2 * x_at[d] + half) for d in range(4)]
-    verticals = [at(s * GRID_W + e, kern) for s in (1, -1) for e in (-1, 0, 1)]
     sign = 2 * (x % 2) - 1
     crossed = 2 * (x + 1 - 2 * (x % 2)) + half
-    crosses = [at(sign * GRID_W + e, crossed) for e in (-1, 0, 1)]
+    near_tiles = [1, -1] + [s * GRID_W + e for s in (1, -1) for e in (-1, 0, 1)]
+    partners = [(valid(by), at(by, kern)) for by in near_tiles]
+    partners += [(valid(by), at(by, crossed)) for by in (sign * GRID_W + e for e in (-1, 0, 1))]
 
     barrier = pltpu.get_barrier_semaphore()
-    partners = verticals + [right, left, far] + peers[1:] + crosses
-    for one in partners:
+    expected = 4
+    for there, one in partners:
+        expected = expected + there.astype(jnp.int32)
+
+        @pl.when(there)
+        def _():
+            pl.semaphore_signal(barrier, inc=1, device_id=one, device_id_type=MESH)
+
+    for one in [far] + peers[1:]:
         pl.semaphore_signal(barrier, inc=1, device_id=one, device_id_type=MESH)
 
     loads = [
         pltpu.make_async_copy(src, dst, load_sem.at[n])
-        for n, (src, dst) in enumerate(((mask_hbm, mask), (kernels_hbm, kernels), (tab_hbm, tab), (target_hbm, target)))
-    ]
-    for copy in loads:
+        for n, (src, dst) in enumerate((
+            (mask_hbm, mask), (kernels_hbm, kernels), (tab_hbm, tab), (target_hbm, target),
+            (link_hbm, link), (weight_hbm, weight),
+        ))
+    ]
+    for copy in (loads[0], loads[4], loads[5], loads[1], loads[2], loads[3]):
         copy.start()
     started = []
 
-    def remote(src, dst, send, recv, device):
+    def remote(src, dst, send, recv, device, there=None):
         copy = pltpu.make_async_remote_copy(
             src_ref=src, dst_ref=dst, send_sem=send, recv_sem=recv, device_id=device, device_id_type=MESH
         )
-        copy.start()
-        started.append(copy)
+        if there is None:
+            copy.start()
+        else:
+            pl.when(there)(copy.start)
+        started.append((there, copy))
         return copy
 
-    lane = lax.broadcasted_iota(jnp.int32, (BLK, BLK), 1) < HALO
-    lane_all = lax.broadcasted_iota(jnp.int32, (CORE, BLK), 1) < HALO
-    lane_part = lax.broadcasted_iota(jnp.int32, (PART, BLK), 1) < HALO
+    def clear_unless(there, *refs):
+        @pl.when(jnp.logical_not(there))
+        def _():
+            for ref in refs:
+                ref[...] = jnp.zeros(ref.shape, F32)
+
+    from_left_tile, from_right_tile = valid(-1), valid(1)
+    from_vert = [valid(-GRID_W), valid(GRID_W)]
+    from_corner = [valid(-GRID_W - 1), valid(-GRID_W + 1), valid(GRID_W - 1), valid(GRID_W + 1)]
+    clear_unless(from_left_tile, side_in.at[0], edge_in.at[0])
+    clear_unless(from_right_tile, side_in.at[1], edge_in.at[1])
+    for n in range(2):
+        clear_unless(from_vert[n], vert_in.at[n])
+    for n in range(4):
+        clear_unless(from_corner[n], corner_in.at[n])
 
     loads[0].wait()
     a0, a1 = mask[0, :, pl.ds(0, BLK)], mask[0, :, pl.ds(BLK, BLK)]
     r0, r1 = pltpu.roll(a0, HALO, 1), pltpu.roll(a1, HALO, 1)
+    lane_all = low_lanes(CORE)
     outer = jnp.where(lane_all, r1, r0)
     inner = jnp.where(lane_all, r0, r1)
-    flipped = pltpu.roll(outer, HALO, 1)
-    side_out[0] = jnp.where(lane, outer[:BLK], flipped[BLK:]) * right_link
-    side_out[1] = jnp.where(lane, flipped[:BLK], outer[BLK:])
     middle = pl.ds(HALO, CORE)
     ext[middle, pl.ds(BLK, BLK)] = inner
     ext[middle, pl.ds(0, BLK)] = outer
+    loads[4].wait()
+    right_link = link[0, 0].astype(F32) * right_ok
+    down_link = link[0, 1].astype(F32) * down_ok
+    flag = lax.broadcasted_iota(jnp.int32, (8, BLK), 0) < 1
     for n, first in enumerate((CORE - HALO, 0)):
         block = pl.ds(pl.multiple_of(HALO + first + PART * x, PART), PART)
         outer_part = ext[block, pl.ds(0, BLK)]
-        vert_out[n, pl.ds(0, PART), pl.ds(0, BLK)] = outer_part
-        vert_out[n, pl.ds(0, PART), pl.ds(BLK, BLK)] = ext[block, pl.ds(BLK, BLK)]
-        vert_out[n, pl.ds(PART, 8), pl.ds(0, BLK)] = jnp.full((8, BLK), down_link, F32)
-        vert_out[n, pl.ds(PART, 8), pl.ds(BLK, BLK)] = jnp.full((8, BLK), right_link, F32)
-        corner_out[n, 0] = outer_part
-        corner_out[n, 1] = outer_part * right_link
-
-    pl.semaphore_wait(barrier, len(partners))
+        vert_out[n, pl.ds(0, PART), :] = outer_part
+        vert_out[n, pl.ds(PART, PART), :] = ext[block, pl.ds(BLK, BLK)]
+        vert_out[n, pl.ds(2 * PART, 8), :] = jnp.where(flag, down_link, right_link)
+        corner_out[n, 0] = pack_high(outer_part)
+        corner_out[n, 1] = pack_low(outer_part) * right_link
+    side_out[0] = pack_low(outer) * right_link
+    side_out[1] = pack_high(outer)
+
+    pl.semaphore_wait(barrier, expected)
+    w = GRID_W
     verts = [
-        remote(vert_out.at[0], vert_in.at[0], vert_send.at[0], vert_recv.at[0], verticals[1]),
-        remote(vert_out.at[1], vert_in.at[1], vert_send.at[1], vert_recv.at[1], verticals[4]),
-        remote(corner_out.at[0, 1], corner_in.at[0], corner_send.at[0], corner_recv.at[0], verticals[2]),
-        remote(corner_out.at[0, 0], corner_in.at[1], corner_send.at[1], corner_recv.at[1], verticals[0]),
-        remote(corner_out.at[1, 1], corner_in.at[2], corner_send.at[2], corner_recv.at[2], verticals[5]),
-        remote(corner_out.at[1, 0], corner_in.at[3], corner_send.at[3], corner_recv.at[3], verticals[3]),
-    ]
+        remote(vert_out.at[0], vert_in.at[0], vert_send.at[0], vert_recv.at[0], at(w, kern), valid(w)),
+        remote(vert_out.at[1], vert_in.at[1], vert_send.at[1], vert_recv.at[1], at(-w, kern), valid(-w)),
+    ]
+    for n, (by, src) in enumerate((
+        (w + 1, corner_out.at[0, 1]), (w - 1, corner_out.at[0, 0]),
+        (1 - w, corner_out.at[1, 1]), (-1 - w, corner_out.at[1, 0]),
+    )):
+        verts.append(remote(src, corner_in.at[n], corner_send.at[n], corner_recv.at[n], at(by, kern), valid(by)))
     sides = [
-        remote(side_out.at[0], side_in.at[0], side_send.at[0], side_recv.at[0], right),
-        remote(side_out.at[1], side_in.at[1], side_send.at[1], side_recv.at[1], left),
+        remote(side_out.at[0], side_in.at[0], side_send.at[0], side_recv.at[0], at(1, kern), valid(1)),
+        remote(side_out.at[1], side_in.at[1], side_send.at[1], side_recv.at[1], at(-1, kern), valid(-1)),
     ]
 
     loads[1].wait()
+    loads[5].wait()
     taps = [[jnp.sum(kernels[c, k], keepdims=True) for k in range(3)] for c in range(2)]
     clear_part = sum(weight[k] * (taps[0][k] * taps[0][k] + taps[1][k] * taps[1][k]) for k in range(3))
     clear_in[x] = jnp.broadcast_to(clear_part, (8, BLK))
@@ -362,25 +422,24 @@
     response_rows(kernels, tab, mid)
     response_cols(0, tab, mid, resp)
 
-    for copy in sides:
-        copy.wait_recv()
-    from_left, from_right = side_in[0], side_in[1] * right_link
-    upper, lower = pl.ds(HALO, BLK), pl.ds(HALO + BLK, BLK)
-    up_outer, low_outer = ext[upper, pl.ds(0, BLK)], ext[lower, pl.ds(0, BLK)]
-    ext[upper, pl.ds(0, BLK)] = jnp.where(lane, from_left, up_outer)
-    ext[lower, pl.ds(0, BLK)] = jnp.where(lane, pltpu.roll(from_left, HALO, 1), low_outer)
-    ext[upper, pl.ds(CORE, BLK)] = jnp.where(lane, up_outer, pltpu.roll(from_right, HALO, 1))
-    ext[lower, pl.ds(CORE, BLK)] = jnp.where(lane, low_outer, from_right)
-
-    for copy in verts:
-        copy.wait_recv()
-    down_above, right_above = vert_in[0, pl.ds(PART, 1), pl.ds(0, 1)], vert_in[0, pl.ds(PART, 1), pl.ds(BLK, 1)]
-    right_below = vert_in[1, pl.ds(PART, 1), pl.ds(BLK, 1)]
+    for there, copy in zip((from_left_tile, from_right_tile), sides):
+        pl.when(there)(copy.wait_recv)
+    from_left, from_right = unpack_low(side_in[0]), unpack_high(side_in[1]) * right_link
+    outer = ext[middle, pl.ds(0, BLK)]
+    ext[middle, pl.ds(0, BLK)] = jnp.where(lane_all, from_left, outer)
+    ext[middle, pl.ds(CORE, BLK)] = jnp.where(lane_all, outer, from_right)
+
+    for there, copy in zip(from_vert + from_corner, verts):
+        pl.when(there)(copy.wait_recv)
+    down_above, right_above = (vert_in[0, pl.ds(2 * PART + r, 1), pl.ds(0, 1)] for r in (0, 1))
+    right_below = vert_in[1, pl.ds(2 * PART + 1, 1), pl.ds(0, 1)]
+    lane_part = low_lanes(PART)
     for n, (factor, beside) in enumerate(((down_above, right_above), (down_link, right_below))):
-        edge = vert_in[n, pl.ds(0, PART), pl.ds(0, BLK)]
-        margin[x, n, :, pl.ds(0, BLK)] = jnp.where(lane_part, corner_in[2 * n], edge) * factor
-        margin[x, n, :, pl.ds(BLK, BLK)] = vert_in[n, pl.ds(0, PART), pl.ds(BLK, BLK)] * factor
-        margin[x, n, :, pl.ds(CORE, BLK)] = jnp.where(lane_part, edge, corner_in[2 * n + 1] * beside) * factor
+        edge = vert_in[n, pl.ds(0, PART), :]
+        first, last = unpack_low(corner_in[2 * n]), unpack_high(corner_in[2 * n + 1])
+        margin[x, n, :, pl.ds(0, BLK)] = jnp.where(lane_part, first, edge) * factor
+        margin[x, n, :, pl.ds(BLK, BLK)] = vert_in[n, pl.ds(PART, PART), :] * factor
+        margin[x, n, :, pl.ds(CORE, BLK)] = jnp.where(lane_part, edge, last * beside) * factor
     shares = [
         remote(margin.at[x], margin.at[x], share_send.at[d - 1], share_recv.at[d - 1], peers[d])
         for d in range(1, 4)
@@ -443,7 +502,7 @@
         wanted = target[0, block, :].astype(F32)
         slope = (4.0 * STEEP) * (printed - wanted) * printed * (1.0 - printed) / clear
         source_cols(h, slope, weight, tab, field, wide)
-    store = pltpu.make_async_copy(resist, resist_out, store_sem.at[0])
+    store = pltpu.make_async_copy(resist, out.at[0], store_sem.at[0])
     store.start()
     for pair in PAIRS:
         source_rows(pair, resp, tab, wide, acc)
@@ -472,57 +531,58 @@
     is_low = jnp.where(low_x, 1.0, 0.0)
     down_factor = is_low * down_link + (1.0 - is_low) * down_above
     right_factor = is_low * right_below + (1.0 - is_low) * right_above
-    fold_out[...] = (halo_parts[x] + halo_in[0] + halo_in[1] + halo_in[2]) * down_factor
-    bend_out[0] = fold_out[:, pl.ds(0, BLK)]
-    bend_out[1] = fold_out[:, pl.ds(CORE, BLK)] * right_factor
+    total = (halo_parts[x] + halo_in[0] + halo_in[1] + halo_in[2]) * down_factor
+    first, last, fold_out[...] = core_blocks(total)
+    bend_out[0] = pack_high(first)
+    bend_out[1] = pack_low(last) * right_factor
     slot = jnp.where((x == 1) | (x == 2), 1, 0)
     step = jnp.where(low_x, GRID_W, -GRID_W)
     owner = jnp.where(low_x, 0, 6) + half
-    folds = [
-        remote(fold_out, fold_in.at[slot], fold_send, fold_recv.at[slot], at(step, owner)),
-        remote(bend_out.at[0], bend_in.at[slot, 0], bend_send.at[0], bend_recv.at[slot, 0], at(step - 1, owner)),
-        remote(bend_out.at[1], bend_in.at[slot, 1], bend_send.at[1], bend_recv.at[slot, 1], at(step + 1, owner)),
-    ]
+    remote(fold_out, fold_in.at[slot], fold_send, fold_recv.at[slot], at(step, owner), valid(step))
+    for n, by in enumerate((step - 1, step + 1)):
+        remote(
+            bend_out.at[n], bend_in.at[slot, n], bend_send.at[n], bend_recv.at[slot, n], at(by, owner), valid(by)
+        )
 
     for copy in core_scatter:
         copy.wait_recv()
-    owned = core_parts[x] + core_in[0] + core_in[1] + core_in[2]
-    edge_out[0] = owned[:, CORE:] * right_link
-    edge_out[1] = owned[:, :BLK]
+    first, last, whole[...] = core_blocks(core_parts[x] + core_in[0] + core_in[1] + core_in[2])
+    edge_out[0] = pack_low(last) * right_link
+    edge_out[1] = pack_high(first)
     edges = [
-        remote(edge_out.at[0], edge_in.at[0], edge_send.at[0], edge_recv.at[0], right),
-        remote(edge_out.at[1], edge_in.at[1], edge_send.at[1], edge_recv.at[1], left),
-    ]
-    core_parts[x] = owned
-
-    @pl.when((x == 0) | (x == 3))
-    def _():
-        for s in range(2):
-            waits = [
-                (fold_out, fold_in.at[s], fold_send, fold_recv.at[s]),
-                (bend_out.at[0], bend_in.at[s, 0], bend_send.at[0], bend_recv.at[s, 0]),
-                (bend_out.at[1], bend_in.at[s, 1], bend_send.at[1], bend_recv.at[s, 1]),
-            ]
-            for src, dst, send, recv in waits:
-                pltpu.make_async_remote_copy(
-                    src_ref=src, dst_ref=dst, send_sem=send, recv_sem=recv, device_id=far, device_id_type=MESH
-                ).wait_recv()
-            block = pl.ds(32 * s, 32)
-            core_parts[x, block, pl.ds(0, BLK)] += fold_in[s, :, pl.ds(0, BLK)] + bend_in[s, 1]
-            core_parts[x, block, pl.ds(BLK, BLK)] += fold_in[s, :, pl.ds(BLK, BLK)]
-            core_parts[x, block, pl.ds(CORE, BLK)] += fold_in[s, :, pl.ds(CORE, BLK)] + bend_in[s, 0] * right_link
-
-    for copy in edges:
-        copy.wait_recv()
-    near_lane = lax.broadcasted_iota(jnp.int32, (QUARTER, BLK), 1) < HALO
-    b0 = core_parts[x, :, pl.ds(0, BLK)] + edge_in[0]
-    b1 = core_parts[x, :, pl.ds(BLK, BLK)]
-    b2 = core_parts[x, :, pl.ds(CORE, BLK)] + edge_in[1] * right_link
-    c0, c1, c2 = (pltpu.roll(b, HALO, 1) for b in (b0, b1, b2))
-    whole = lanes(jnp.where(near_lane, c0, c1), jnp.where(near_lane, c1, c2))
+        remote(edge_out.at[0], edge_in.at[0], edge_send.at[0], edge_recv.at[0], at(1, kern), valid(1)),
+        remote(edge_out.at[1], edge_in.at[1], edge_send.at[1], edge_recv.at[1], at(-1, kern), valid(-1)),
+    ]
+
+    takes = (x == 0) | (x == 3)
+    back = jnp.where(x == 0, -GRID_W, GRID_W)
+    lane_fold = low_lanes(32)
+    for s in range(2):
+        arrivals = (
+            (valid(back), fold_out, fold_in.at[s], fold_send, fold_recv.at[s]),
+            (valid(back + 1), bend_out.at[0], bend_in.at[s, 0], bend_send.at[0], bend_recv.at[s, 0]),
+            (valid(back - 1), bend_out.at[1], bend_in.at[s, 1], bend_send.at[1], bend_recv.at[s, 1]),
+        )
+        for there, src, dst, send, recv in arrivals:
+            copy = pltpu.make_async_remote_copy(
+                src_ref=src, dst_ref=dst, send_sem=send, recv_sem=recv, device_id=far, device_id_type=MESH
+            )
+            clear_unless(takes & there, dst)
+            pl.when(takes & there)(copy.wait_recv)
+        block = pl.ds(32 * s, 32)
+        from_left = jnp.where(lane_fold, unpack_low(bend_in[s, 1]), 0.0)
+        from_right = jnp.where(lane_fold, 0.0, unpack_high(bend_in[s, 0])) * right_link
+        whole[block, :] += fold_in[s] + lanes(from_left, from_right)
+
+    for there, copy in zip((from_left_tile, from_right_tile), edges):
+        pl.when(there)(copy.wait_recv)
+    lane_edge = low_lanes(QUARTER)
+    from_left = jnp.where(lane_edge, unpack_low(edge_in[0]), 0.0)
+    from_right = jnp.where(lane_edge, 0.0, unpack_high(edge_in[1])) * right_link
+    partial = whole[...] + lanes(from_left, from_right)
     swaps = []
     for h in range(2):
-        mine[h] = whole[h * 32 : (h + 1) * 32]
+        mine[h] = partial[h * 32 : (h + 1) * 32]
         swaps.append(remote(mine.at[h], other.at[h], gfar_send.at[h], gfar_recv.at[h], far))
     finals = []
     for h in range(2):
@@ -540,19 +600,21 @@
         for h in range(2):
             stores.append(
                 pltpu.make_async_copy(
-                    gathered.at[q, h], grad_out.at[0, pl.ds(64 * q + 32 * h, 32)], store_sem.at[1 + 2 * q + h]
+                    gathered.at[q, h], out.at[1, 0, pl.ds(64 * q + 32 * h, 32)], store_sem.at[1 + 2 * q + h]
                 )
             )
             stores[-1].start()
-    for copy in started:
-        copy.wait_send()
+    for there, copy in started:
+        if there is None:
+            copy.wait_send()
+        else:
+            pl.when(there)(copy.wait_send)
     store.wait()
     for copy in stores:
         copy.wait()
 
 
 def body(mask, kernels, weight, link, target):
-    smem = pl.BlockSpec(memory_space=pltpu.SMEM)
     anywhere = pl.BlockSpec(memory_space=pl.ANY)
     dma = pltpu.SemaphoreType.DMA
     f32 = lambda *shape: pltpu.VMEM(shape, F32)
@@ -561,32 +623,32 @@
         pltpu.VMEM((2, 2, 3, CORE, CORE), BF16),
         f32(2, EXTENT, EXTENT), f32(2, CORE, 3 * EXTENT), f32(2, EXTENT, 3 * EXTENT), f32(2, EXTENT, EXTENT),
         f32(2, 2, EXTENT, CORE), f32(2, EXTENT, EXTENT), f32(EXTENT, EXTENT), f32(1, CORE, CORE),
-        f32(2, BLK, BLK), f32(2, BLK, BLK), f32(2, PART + 8, CORE), f32(2, PART + 8, CORE),
-        f32(2, 2, PART, BLK), f32(4, PART, BLK), f32(4, 2, PART, EXTENT),
+        f32(2, BLK, BLK), f32(2, BLK, BLK), f32(2, 2 * PART + 8, BLK), f32(2, 2 * PART + 8, BLK),
+        f32(2, 2, PART // 2, BLK), f32(4, PART // 2, BLK), f32(4, 2, PART, EXTENT),
         f32(4, 8, BLK), f32(8, BLK), f32(8, BLK),
         f32(2, 4, EIGHTH, CORE), f32(2, 3, EIGHTH, CORE), f32(2, EIGHTH, CORE), f32(2, EIGHTH, CORE),
         f32(2, 4, EIGHTH, CORE),
         f32(4, 32, EXTENT), f32(3, 32, EXTENT), f32(4, QUARTER, EXTENT), f32(3, QUARTER, EXTENT),
-        f32(32, EXTENT), f32(2, 32, EXTENT), f32(2, 32, BLK), f32(2, 2, 32, BLK),
-        f32(2, QUARTER, BLK), f32(2, QUARTER, BLK),
+        f32(32, CORE), f32(2, 32, CORE), f32(2, 16, BLK), f32(2, 2, 16, BLK),
+        f32(2, 32, BLK), f32(2, 32, BLK), f32(QUARTER, CORE),
         f32(2, 32, CORE), f32(2, 32, CORE), f32(4, 2, 32, CORE),
     ]
-    sems = [dma((4,)), dma((9,))] + [dma((2,))] * 4 + [dma((4,))] * 2 + [dma((3,))] * 2
+    sems = [pltpu.SMEM((3,), F32), pltpu.SMEM((1, 2), jnp.int32), dma((6,)), dma((9,))] + [dma((2,))] * 4 + [dma((4,))] * 2 + [dma((3,))] * 2
     sems += [dma((3,))] * 2 + [dma] * 2
     sems += [dma((2, 3))] * 2 + [dma((2,))] * 2 + [dma((2, 3))] * 2
     sems += [dma((3,))] * 4 + [dma, dma((2,)), dma((2,)), dma((2, 2))]
     sems += [dma((2,))] * 4 + [dma((2, 3))] * 2
-    out = jax.ShapeDtypeStruct((1, CORE, CORE), F32)
-    return pl.pallas_call(
+    both = pl.pallas_call(
         body_kernel,
-        out_shape=(out, out),
-        in_specs=[anywhere] * 4 + [smem] * 2,
-        out_specs=(anywhere, anywhere),
+        out_shape=jax.ShapeDtypeStruct((2, 1, CORE, CORE), F32),
+        in_specs=[anywhere] * 6,
+        out_specs=anywhere,
         scratch_shapes=buffers + sems,
         compiler_params=pltpu.CompilerParams(
             collective_id=0, has_side_effects=True, vmem_limit_bytes=60 * 2**20
         ),
     )(mask, kernels, target, jnp.asarray(dft_tables()), weight, link)
+    return both[0], both[1]
 
 
 def solution(mesh):

time: 73.8 us -> 69.8 us (0.946)
  the two profiles are of different devices: /device:TPU:1 before, /device:TPU:50 now
where the time goes in v2:
time: 69.8 us; the launch traced here: 69.6 us
  Pallas kernels  67.1 us (96%)
  local copies, waits for them, and re-layouts  1.85 us (3%)
    pallas_call x1, Pallas kernels, body(): pl.pallas_call(body_kernel, out_shape=jax.ShapeDtypeStruct((2, 1, CORE, C...  67.1 us
    squeeze x1, local copies, waits for them, and re-layouts, body(): return (both[0], both[1])  1.85 us

profile of v2, /device:TPU:50, one launch (start us, length us, event | category | flops | bytes accessed | tf_op | source)
XLA Modules:
  0.0 69.6 jit_solution(4719319462995248793)
XLA Ops:
  0.6 67.1 %shard_map.77 = f32[2,1,256,256]{3,2,1,0:T(8,128)} custom-call(f32[1,256,256]{2,1,0:T(8,128)} %mask_hbm.1, f32[2,3,128,128]{3,2,1,0:T(8,128)} %kernels_hbm.1, s32[1,256,256]{2,1,0:T(8,128)} %target_hbm.1, bf16[2,2,3,256,256]{4,3,2,1,0:T(8,128)(2,1)} %constant.2.clone.tab_hbm, f32[3]{0:T(128)} %weight_hbm.1, s32[1,2]{1,0:T(1,128)} %link_hbm.1), custom_call_target="tpu_custom_call" | custom-call | tf_op jit(solution)/shard_map/pallas_call | solution.py:641
  67.8 1.9 %slice_bitcast_fusion = (f32[1,256,256]{2,1,0:T(8,128)}, f32[1,256,256]{2,1,0:T(8,128)}) fusion(f32[2,1,256,256]{3,2,1,0:T(8,128)} %shard_map.77), kind=kLoop, calls=%fused_computation | loop fusion | bytes 1048576 | tf_op jit(solution)/shard_map/squeeze | solution.py:651

commit v3 on v2

--- a/solution.py
+++ b/solution.py
@@ -54,7 +54,9 @@
 
 def mul_left(high, low, x):
     xh, xl = split(x)
-    return dot(high, xh) + (dot(low, xh) + dot(high, xl))
+    n = x.shape[1]
+    both = dot(high, jnp.concatenate([xh, xl], axis=1))
+    return both[:, :n] + (both[:, n:] + dot(low, xh))
 
 
 def fwd_mat(tab, g):
@@ -252,6 +254,7 @@
 QUARTER = CORE // 4
 EIGHTH = CORE // 8
 PART = HALO // 4
+FARTHEST_FIRST = (2, 1, 3)
 
 
 def low_lanes(n):
@@ -352,6 +355,14 @@
             pl.when(there)(copy.start)
         started.append((there, copy))
         return copy
+
+    def finish_sends():
+        for there, copy in started:
+            if there is None:
+                copy.wait_send()
+            else:
+                pl.when(there)(copy.wait_send)
+        started.clear()
 
     def clear_unless(there, *refs):
         @pl.when(jnp.logical_not(there))
@@ -416,7 +427,7 @@
     clear_in[x] = jnp.broadcast_to(clear_part, (8, BLK))
     clears = [
         remote(clear_in.at[x], clear_in.at[x], clear_send.at[d - 1], clear_recv.at[d - 1], peers[d])
-        for d in range(1, 4)
+        for d in FARTHEST_FIRST
     ]
     loads[2].wait()
     response_rows(kernels, tab, mid)
@@ -442,7 +453,7 @@
         margin[x, n, :, pl.ds(CORE, BLK)] = jnp.where(lane_part, edge, last * beside) * factor
     shares = [
         remote(margin.at[x], margin.at[x], share_send.at[d - 1], share_recv.at[d - 1], peers[d])
-        for d in range(1, 4)
+        for d in FARTHEST_FIRST
     ]
     for copy in clears:
         copy.wait_recv()
@@ -473,7 +484,7 @@
             power[h, q] = p
         scatter.append([
             remote(power.at[h, x_at[d]], power_in.at[h, d - 1], psc_send.at[h, d - 1], psc_recv.at[h, d - 1], peers[d])
-            for d in range(1, 4)
+            for d in FARTHEST_FIRST
         ])
     loads[3].wait()
     clear_copy.wait_recv()
@@ -483,13 +494,14 @@
             copy.wait_recv()
         power_mine[h] = power[h, x] + power_in[h, 0] + power_in[h, 1] + power_in[h, 2]
         swaps.append(remote(power_mine.at[h], power_far.at[h], pfar_send.at[h], pfar_recv.at[h], far))
+    finish_sends()
     gathers = []
     for h in range(2):
         swaps[h].wait_recv()
         power_all[h, x] = power_mine[h] + power_far[h]
         gathers.append([
             remote(power_all.at[h, x], power_all.at[h, x], pall_send.at[h, d - 1], pall_recv.at[h, d - 1], peers[d])
-            for d in range(1, 4)
+            for d in FARTHEST_FIRST
         ])
     clear = (clear_sum[...] + clear_far[...])[0:1, 0:1]
     for h in range(2):
@@ -514,7 +526,7 @@
             halo_parts[q, :, pl.ds(c * BLK, BLK)] = blocks[c][start : start + 32]
     halo_scatter = [
         remote(halo_parts.at[x_at[d]], halo_in.at[d - 1], hsc_send.at[d - 1], hsc_recv.at[d - 1], peers[d])
-        for d in range(1, 4)
+        for d in FARTHEST_FIRST
     ]
     blocks = gradient_cols([(HALO, CORE)], tab, mid)
     for c in range(3):
@@ -522,7 +534,7 @@
             core_parts[q, :, pl.ds(c * BLK, BLK)] = blocks[c][q * QUARTER : (q + 1) * QUARTER]
     core_scatter = [
         remote(core_parts.at[x_at[d]], core_in.at[d - 1], gsc_send.at[d - 1], gsc_recv.at[d - 1], peers[d])
-        for d in range(1, 4)
+        for d in FARTHEST_FIRST
     ]
 
     low_x = x < 2
@@ -584,32 +596,40 @@
     for h in range(2):
         mine[h] = partial[h * 32 : (h + 1) * 32]
         swaps.append(remote(mine.at[h], other.at[h], gfar_send.at[h], gfar_recv.at[h], far))
+    finish_sends()
     finals = []
+    stores = [store]
     for h in range(2):
         swaps[h].wait_recv()
-        gathered[x, h] = mine[h] + other[h]
-        finals.append([
-            remote(gathered.at[x, h], gathered.at[x, h], all_send.at[h, d - 1], all_recv.at[h, d - 1], peers[d])
-            for d in range(1, 4)
-        ])
-    for h in range(2):
-        for copy in finals[h]:
-            copy.wait_recv()
+        gathered[h] = mine[h] + other[h]
+        place = out.at[1, 0, pl.ds(pl.multiple_of(QUARTER * x + 32 * h, 32), 32)]
+        finals += [
+            remote(gathered.at[h], place, all_send.at[h, d - 1], all_recv.at[h, d - 1], peers[d])
+            for d in FARTHEST_FIRST
+        ]
+        stores.append(pltpu.make_async_copy(gathered.at[h], place, store_sem.at[1 + h]))
+        stores[-1].start()
+    for copy in finals:
+        copy.wait_recv()
+    finish_sends()
+    for copy in stores:
+        copy.wait()
+
+
+def store_kernel(both, resist_out, grad_out, held, load_sem, store_sem):
+    pieces = [(n, pl.ds(q * BLK, BLK)) for n in range(2) for q in range(2)]
+    loads = [
+        pltpu.make_async_copy(both.at[n, 0, block], held.at[n, 0, block], load_sem.at[i])
+        for i, (n, block) in enumerate(pieces)
+    ]
+    for copy in loads:
+        copy.start()
     stores = []
-    for q in range(4):
-        for h in range(2):
-            stores.append(
-                pltpu.make_async_copy(
-                    gathered.at[q, h], out.at[1, 0, pl.ds(64 * q + 32 * h, 32)], store_sem.at[1 + 2 * q + h]
-                )
-            )
-            stores[-1].start()
-    for there, copy in started:
-        if there is None:
-            copy.wait_send()
-        else:
-            pl.when(there)(copy.wait_send)
-    store.wait()
+    for i, (n, block) in enumerate(pieces):
+        loads[i].wait()
+        into = (resist_out, grad_out)[n]
+        stores.append(pltpu.make_async_copy(held.at[n, 0, block], into.at[0, block], store_sem.at[i]))
+        stores[-1].start()
     for copy in stores:
         copy.wait()
 
@@ -631,9 +651,9 @@
         f32(4, 32, EXTENT), f32(3, 32, EXTENT), f32(4, QUARTER, EXTENT), f32(3, QUARTER, EXTENT),
         f32(32, CORE), f32(2, 32, CORE), f32(2, 16, BLK), f32(2, 2, 16, BLK),
         f32(2, 32, BLK), f32(2, 32, BLK), f32(QUARTER, CORE),
-        f32(2, 32, CORE), f32(2, 32, CORE), f32(4, 2, 32, CORE),
-    ]
-    sems = [pltpu.SMEM((3,), F32), pltpu.SMEM((1, 2), jnp.int32), dma((6,)), dma((9,))] + [dma((2,))] * 4 + [dma((4,))] * 2 + [dma((3,))] * 2
+        f32(2, 32, CORE), f32(2, 32, CORE), f32(2, 32, CORE),
+    ]
+    sems = [pltpu.SMEM((3,), F32), pltpu.SMEM((1, 2), jnp.int32), dma((6,)), dma((3,))] + [dma((2,))] * 4 + [dma((4,))] * 2 + [dma((3,))] * 2
     sems += [dma((3,))] * 2 + [dma] * 2
     sems += [dma((2, 3))] * 2 + [dma((2,))] * 2 + [dma((2, 3))] * 2
     sems += [dma((3,))] * 4 + [dma, dma((2,)), dma((2,)), dma((2, 2))]
@@ -648,7 +668,15 @@
             collective_id=0, has_side_effects=True, vmem_limit_bytes=60 * 2**20
         ),
     )(mask, kernels, target, jnp.asarray(dft_tables()), weight, link)
-    return both[0], both[1]
+    out = jax.ShapeDtypeStruct((1, CORE, CORE), F32)
+    return pl.pallas_call(
+        store_kernel,
+        out_shape=(out, out),
+        in_specs=[anywhere],
+        out_specs=(anywhere, anywhere),
+        scratch_shapes=[f32(2, 1, CORE, CORE), dma((4,)), dma((4,))],
+        compiler_params=pltpu.CompilerParams(vmem_limit_bytes=60 * 2**20),
+    )(both)
 
 
 def solution(mesh):

time: 69.8 us -> 67.7 us (0.970)
  the two profiles are of different devices: /device:TPU:50 before, /device:TPU:11 now
where the time goes in v3:
time: 67.7 us; the launch traced here: 67.5 us
  Pallas kernels  66.9 us (99%)
    pallas_call x1, Pallas kernels, body(): pl.pallas_call(body_kernel, out_shape=jax.ShapeDtypeStruct((2, 1, CORE, C...  65.1 us
    pallas_call x1, Pallas kernels, body(): pl.pallas_call(store_kernel, out_shape=(out, out), in_specs=[anywhere], o...  1.82 us

profile of v3, /device:TPU:11, one launch (start us, length us, event | category | flops | bytes accessed | tf_op | source)
XLA Modules:
  0.0 67.5 jit_solution(8743059199253136498)
XLA Ops:
  0.6 65.1 %shard_map.77.both = f32[2,1,256,256]{3,2,1,0:T(8,128)} custom-call(f32[1,256,256]{2,1,0:T(8,128)} %mask_hbm.1, f32[2,3,128,128]{3,2,1,0:T(8,128)} %kernels_hbm.1, s32[1,256,256]{2,1,0:T(8,128)} %target_hbm.1, bf16[2,2,3,256,256]{4,3,2,1,0:T(8,128)(2,1)} %constant.2.clone.tab_hbm, f32[3]{0:T(128)} %weight_hbm.1, s32[1,2]{1,0:T(1,128)} %link_hbm.1), custom_call_target="tpu_custom_call" | custom-call | tf_op jit(solution)/shard_map/pallas_call | solution.py:661
  65.7 1.8 %shard_map.78 = (f32[1,256,256]{2,1,0:T(8,128)}, f32[1,256,256]{2,1,0:T(8,128)}) custom-call(f32[2,1,256,256]{3,2,1,0:T(8,128)} %shard_map.77.both), custom_call_target="tpu_custom_call" | custom-call | tf_op jit(solution)/shard_map/pallas_call | solution.py:672

commit v4 on v3

--- a/solution.py
+++ b/solution.py
@@ -254,7 +254,7 @@
 QUARTER = CORE // 4
 EIGHTH = CORE // 8
 PART = HALO // 4
-FARTHEST_FIRST = (2, 1, 3)
+FARTHEST_FIRST = (2, 3, 1)
 
 
 def low_lanes(n):
@@ -295,7 +295,7 @@
     weight, link, load_sem, store_sem, side_send, side_recv, vert_send, vert_recv, corner_send, corner_recv, share_send, share_recv,
     clear_send, clear_recv, cfar_send, cfar_recv,
     psc_send, psc_recv, pfar_send, pfar_recv, pall_send, pall_recv,
-    hsc_send, hsc_recv, gsc_send, gsc_recv, fold_send, fold_recv, bend_send, bend_recv,
+    hsc_send, hsc_recv, gsc_send, gsc_recv, gmid_send, gmid_recv, fold_send, fold_recv, bend_send, bend_recv,
     edge_send, edge_recv, gfar_send, gfar_recv, all_send, all_recv,
 ):
     tile = lax.axis_index("tile")
@@ -406,6 +406,10 @@
 
     pl.semaphore_wait(barrier, expected)
     w = GRID_W
+    sides = [
+        remote(side_out.at[0], side_in.at[0], side_send.at[0], side_recv.at[0], at(1, kern), valid(1)),
+        remote(side_out.at[1], side_in.at[1], side_send.at[1], side_recv.at[1], at(-1, kern), valid(-1)),
+    ]
     verts = [
         remote(vert_out.at[0], vert_in.at[0], vert_send.at[0], vert_recv.at[0], at(w, kern), valid(w)),
         remote(vert_out.at[1], vert_in.at[1], vert_send.at[1], vert_recv.at[1], at(-w, kern), valid(-w)),
@@ -415,10 +419,6 @@
         (1 - w, corner_out.at[1, 1]), (-1 - w, corner_out.at[1, 0]),
     )):
         verts.append(remote(src, corner_in.at[n], corner_send.at[n], corner_recv.at[n], at(by, kern), valid(by)))
-    sides = [
-        remote(side_out.at[0], side_in.at[0], side_send.at[0], side_recv.at[0], at(1, kern), valid(1)),
-        remote(side_out.at[1], side_in.at[1], side_send.at[1], side_recv.at[1], at(-1, kern), valid(-1)),
-    ]
 
     loads[1].wait()
     loads[5].wait()
@@ -529,11 +529,19 @@
         for d in FARTHEST_FIRST
     ]
     blocks = gradient_cols([(HALO, CORE)], tab, mid)
-    for c in range(3):
+    for n, c in enumerate((0, 2, 1)):
         for q in range(4):
-            core_parts[q, :, pl.ds(c * BLK, BLK)] = blocks[c][q * QUARTER : (q + 1) * QUARTER]
+            core_parts[q, n] = blocks[c][q * QUARTER : (q + 1) * QUARTER]
+    outer_blocks = pl.ds(0, 2)
     core_scatter = [
-        remote(core_parts.at[x_at[d]], core_in.at[d - 1], gsc_send.at[d - 1], gsc_recv.at[d - 1], peers[d])
+        remote(
+            core_parts.at[x_at[d], outer_blocks], core_in.at[d - 1, outer_blocks],
+            gsc_send.at[d - 1], gsc_recv.at[d - 1], peers[d],
+        )
+        for d in FARTHEST_FIRST
+    ]
+    middle_scatter = [
+        remote(core_parts.at[x_at[d], 2], core_in.at[d - 1, 2], gmid_send.at[d - 1], gmid_recv.at[d - 1], peers[d])
         for d in FARTHEST_FIRST
     ]
 
@@ -558,7 +566,9 @@
 
     for copy in core_scatter:
         copy.wait_recv()
-    first, last, whole[...] = core_blocks(core_parts[x] + core_in[0] + core_in[1] + core_in[2])
+    first, last = (
+        pltpu.roll(core_parts[x, n] + core_in[0, n] + core_in[1, n] + core_in[2, n], HALO, 1) for n in (0, 1)
+    )
     edge_out[0] = pack_low(last) * right_link
     edge_out[1] = pack_high(first)
     edges = [
@@ -566,6 +576,11 @@
         remote(edge_out.at[1], edge_in.at[1], edge_send.at[1], edge_recv.at[1], at(-1, kern), valid(-1)),
     ]
 
+    for copy in middle_scatter:
+        copy.wait_recv()
+    between = pltpu.roll(core_parts[x, 2] + core_in[0, 2] + core_in[1, 2] + core_in[2, 2], HALO, 1)
+    lane_edge = low_lanes(QUARTER)
+    whole[...] = lanes(jnp.where(lane_edge, first, between), jnp.where(lane_edge, between, last))
     takes = (x == 0) | (x == 3)
     back = jnp.where(x == 0, -GRID_W, GRID_W)
     lane_fold = low_lanes(32)
@@ -588,7 +603,6 @@
 
     for there, copy in zip((from_left_tile, from_right_tile), edges):
         pl.when(there)(copy.wait_recv)
-    lane_edge = low_lanes(QUARTER)
     from_left = jnp.where(lane_edge, unpack_low(edge_in[0]), 0.0)
     from_right = jnp.where(lane_edge, 0.0, unpack_high(edge_in[1])) * right_link
     partial = whole[...] + lanes(from_left, from_right)
@@ -648,7 +662,7 @@
         f32(4, 8, BLK), f32(8, BLK), f32(8, BLK),
         f32(2, 4, EIGHTH, CORE), f32(2, 3, EIGHTH, CORE), f32(2, EIGHTH, CORE), f32(2, EIGHTH, CORE),
         f32(2, 4, EIGHTH, CORE),
-        f32(4, 32, EXTENT), f32(3, 32, EXTENT), f32(4, QUARTER, EXTENT), f32(3, QUARTER, EXTENT),
+        f32(4, 32, EXTENT), f32(3, 32, EXTENT), f32(4, 3, QUARTER, BLK), f32(3, 3, QUARTER, BLK),
         f32(32, CORE), f32(2, 32, CORE), f32(2, 16, BLK), f32(2, 2, 16, BLK),
         f32(2, 32, BLK), f32(2, 32, BLK), f32(QUARTER, CORE),
         f32(2, 32, CORE), f32(2, 32, CORE), f32(2, 32, CORE),
@@ -656,7 +670,7 @@
     sems = [pltpu.SMEM((3,), F32), pltpu.SMEM((1, 2), jnp.int32), dma((6,)), dma((3,))] + [dma((2,))] * 4 + [dma((4,))] * 2 + [dma((3,))] * 2
     sems += [dma((3,))] * 2 + [dma] * 2
     sems += [dma((2, 3))] * 2 + [dma((2,))] * 2 + [dma((2, 3))] * 2
-    sems += [dma((3,))] * 4 + [dma, dma((2,)), dma((2,)), dma((2, 2))]
+    sems += [dma((3,))] * 6 + [dma, dma((2,)), dma((2,)), dma((2, 2))]
     sems += [dma((2,))] * 4 + [dma((2, 3))] * 2
     both = pl.pallas_call(
         body_kernel,

time: 67.7 us -> 67.3 us (level)
  the two profiles are of different devices: /device:TPU:11 before, /device:TPU:1 now
where the time goes in v4:
time: 67.3 us; the launch traced here: 66.9 us
  Pallas kernels  66.3 us (99%)
    pallas_call x1, Pallas kernels, body(): pl.pallas_call(body_kernel, out_shape=jax.ShapeDtypeStruct((2, 1, CORE, C...  64.5 us
    pallas_call x1, Pallas kernels, body(): pl.pallas_call(store_kernel, out_shape=(out, out), in_specs=[anywhere], o...  1.82 us

profile of v4, /device:TPU:1, one launch (start us, length us, event | category | flops | bytes accessed | tf_op | source)
XLA Modules:
  0.0 66.9 jit_solution(8733296616544218675)
XLA Ops:
  0.6 64.5 %shard_map.77.both = f32[2,1,256,256]{3,2,1,0:T(8,128)} custom-call(f32[1,256,256]{2,1,0:T(8,128)} %mask_hbm.1, f32[2,3,128,128]{3,2,1,0:T(8,128)} %kernels_hbm.1, s32[1,256,256]{2,1,0:T(8,128)} %target_hbm.1, bf16[2,2,3,256,256]{4,3,2,1,0:T(8,128)(2,1)} %constant.2.clone.tab_hbm, f32[3]{0:T(128)} %weight_hbm.1, s32[1,2]{1,0:T(1,128)} %link_hbm.1), custom_call_target="tpu_custom_call" | custom-call | tf_op jit(solution)/shard_map/pallas_call | solution.py:675
  65.1 1.8 %shard_map.78 = (f32[1,256,256]{2,1,0:T(8,128)}, f32[1,256,256]{2,1,0:T(8,128)}) custom-call(f32[2,1,256,256]{3,2,1,0:T(8,128)} %shard_map.77.both), custom_call_target="tpu_custom_call" | custom-call | tf_op jit(solution)/shard_map/pallas_call | solution.py:686

commit v5 on v4

--- a/solution.py
+++ b/solution.py
@@ -49,7 +49,9 @@
 
 def mul_right(x, high, low):
     xh, xl = split(x)
-    return dot(xh, high) + (dot(xh, low) + dot(xl, high))
+    n = high.shape[1]
+    both = dot(xh, jnp.concatenate([high, low], axis=1))
+    return both[:, :n] + (both[:, n:] + dot(xl, high))
 
 
 def mul_left(high, low, x):
@@ -132,7 +134,7 @@
     spec[1, pl.ds(2 * BLK, BLK), :] = lanes(out2[BLK:], -out1[BLK:, BLK:])
 
 
-PAIRS = [[(b // 3, b % 3) for b in range(s, min(s + 2, 9))] for s in range(0, 9, 2)]
+PAIRS = [[(b // 3, b % 3) for b in range(s, min(s + 4, 9))] for s in range(0, 9, 4)]
 
 
 def field_rows(pair, resp, spec, tab, mid):

time: 67.3 us -> 67.4 us (level)
  no operation moved by 1% of the time
where the time goes in v5:
time: 67.4 us; the launch traced here: 67 us
  Pallas kernels  66.4 us (99%)
    pallas_call x1, Pallas kernels, body(): pl.pallas_call(body_kernel, out_shape=jax.ShapeDtypeStruct((2, 1, CORE, C...  64.5 us
    pallas_call x1, Pallas kernels, body(): pl.pallas_call(store_kernel, out_shape=(out, out), in_specs=[anywhere], o...  1.82 us

profile of v5, /device:TPU:1, one launch (start us, length us, event | category | flops | bytes accessed | tf_op | source)
XLA Modules:
  0.0 67.0 jit_solution(14327393361868100075)
XLA Ops:
  0.6 64.5 %shard_map.77.both = f32[2,1,256,256]{3,2,1,0:T(8,128)} custom-call(f32[1,256,256]{2,1,0:T(8,128)} %mask_hbm.1, f32[2,3,128,128]{3,2,1,0:T(8,128)} %kernels_hbm.1, s32[1,256,256]{2,1,0:T(8,128)} %target_hbm.1, bf16[2,2,3,256,256]{4,3,2,1,0:T(8,128)(2,1)} %constant.2.clone.tab_hbm, f32[3]{0:T(128)} %weight_hbm.1, s32[1,2]{1,0:T(1,128)} %link_hbm.1), custom_call_target="tpu_custom_call" | custom-call | tf_op jit(solution)/shard_map/pallas_call | solution.py:677
  65.2 1.8 %shard_map.78 = (f32[1,256,256]{2,1,0:T(8,128)}, f32[1,256,256]{2,1,0:T(8,128)}) custom-call(f32[2,1,256,256]{3,2,1,0:T(8,128)} %shard_map.77.both), custom_call_target="tpu_custom_call" | custom-call | tf_op jit(solution)/shard_map/pallas_call | solution.py:688
